TPU v7x, 32 devices: a whole 2x2x4 slice. The times are simulated.
32 devices in a mesh: ctx: 8 (over y, x, core), ch: 4 (over z).
Axes of the slice: x: 2, y: 2, z: 4, core: 2. Of those that a mesh axis runs over, the one named last changes fastest.
Arguments:
- q_vals: bfloat16 [8192, 2048], P('ch', 'ctx'), may hold values from -6 to 6
- k_vals: bfloat16 [8192, 2048], P('ch', 'ctx'), may hold values from -6 to 6
- v_vals: bfloat16 [8192, 2048], P('ch', 'ctx'), may hold values from -6 to 6
- grad_out: bfloat16 [8192, 2048], P('ch', 'ctx'), may hold values from -6 to 6
- exponents: int32 [3, 64, 16], P(None, 'ch', 'ctx'), may hold values from -2 to 1
- filter_taps: float32 [512, 1024], P('ch'), may hold values from -1 to 1
Outputs:
- grad_q: bfloat16 [8192, 2048], P('ch', 'ctx')
- grad_k: bfloat16 [8192, 2048], P('ch', 'ctx')
- grad_v: bfloat16 [8192, 2048], P('ch', 'ctx')
- grad_filter: float32 [512, 1024], P('ch', 'ctx')
- grad_amax: float32 [3, 16], P(None, 'ctx')
All inputs are finite; a program needn't handle non-finite values.
Results may differ from a plain program's by a relative error of at most 0.0061.
Values may be sent and summed in bfloat16 or wider, within the bound.
A program may use at most 128 MiB of HBM per device.

v0:
```python
import jax
import jax.numpy as jnp
from jax import lax
from jax.sharding import PartitionSpec as P

EPS = 1e-06


def expand(scale, scale_rows):
    return jnp.repeat(jnp.repeat(scale, scale_rows, axis=0), scale_rows, axis=1)


def toeplitz_tile(padded_taps, offset, tile_rows):
    groups = padded_taps.shape[0]
    window_vals = lax.dynamic_slice_in_dim(padded_taps, offset * tile_rows + 1, 2 * tile_rows, 1)
    reversed_vals = window_vals[:, ::-1]
    rotated = jnp.concatenate([reversed_vals[:, tile_rows:], reversed_vals[:, :tile_rows]], axis=1)
    repeated = jnp.broadcast_to(rotated[:, None, :], (groups, tile_rows, 2 * tile_rows))
    flat = repeated.reshape(groups, 2 * tile_rows * tile_rows)[:, : tile_rows * (2 * tile_rows - 1)]
    return flat.reshape(groups, tile_rows, 2 * tile_rows - 1)[:, :, :tile_rows]


def convolve(sources, targets, local_grad, filter_taps, tile_rows):
    groups, filter_len = filter_taps.shape
    channels, out_rows = local_grad.shape
    group_width = channels // groups
    out_tiles = out_rows // tile_rows
    lead_tiles = filter_len // tile_rows
    all_tiles = sources.shape[1] // tile_rows
    sources = sources.reshape(groups, group_width, all_tiles, tile_rows)
    targets = targets.reshape(groups, group_width, all_tiles, tile_rows)
    local_grad = local_grad.reshape(groups, group_width, out_tiles, tile_rows)
    padded_taps = jnp.pad(filter_taps.astype(jnp.bfloat16), ((0, 0), (tile_rows, tile_rows + 1)))
    diag_len = 2 * tile_rows - 1

    def one_offset(offset, carry):
        w_acc, gz_acc, lag_acc = carry
        toeplitz = toeplitz_tile(padded_taps, offset, tile_rows)
        z_src = lax.dynamic_slice_in_dim(sources, lead_tiles - offset, out_tiles, 2)
        g_src = lax.dynamic_slice_in_dim(targets, offset, out_tiles, 2)
        w_acc = w_acc + jnp.einsum(
            "gij,gcpj->gcpi", toeplitz, z_src, preferred_element_type=jnp.float32
        )
        gz_acc = gz_acc + jnp.einsum(
            "gji,gcpj->gcpi", toeplitz, g_src, preferred_element_type=jnp.float32
        )
        cross_sum = jnp.einsum(
            "gcpi,gcpj->gij", local_grad, z_src, preferred_element_type=jnp.float32
        )
        flipped = jnp.concatenate([cross_sum[:, :, ::-1], jnp.zeros_like(cross_sum)], axis=2)
        skewed = flipped.reshape(groups, 2 * tile_rows * tile_rows)[:, : tile_rows * diag_len]
        diagonal = jnp.sum(skewed.reshape(groups, tile_rows, diag_len), axis=1)
        offset_at = offset * tile_rows + 1
        current = lax.dynamic_slice_in_dim(lag_acc, offset_at, diag_len, 1)
        lag_acc = lax.dynamic_update_slice_in_dim(lag_acc, current + diagonal, offset_at, 1)
        return (w_acc, gz_acc, lag_acc)

    initial = (
        jnp.zeros((groups, group_width, out_tiles, tile_rows), jnp.float32),
        jnp.zeros((groups, group_width, out_tiles, tile_rows), jnp.float32),
        jnp.zeros((groups, filter_len + 2 * tile_rows), jnp.float32),
    )
    w_acc, gz_acc, lag_acc = lax.fori_loop(0, lead_tiles + 1, one_offset, initial)
    return (
        w_acc.reshape(channels, out_rows),
        gz_acc.reshape(channels, out_rows),
        lag_acc[:, tile_rows : tile_rows + filter_len],
    )


def shards(q_vals, k_vals, v_vals, grad_out, exponents, filter_taps):
    channels, local_rows = q_vals.shape
    groups, filter_len = filter_taps.shape
    group_width = channels // groups
    scale_rows = local_rows // exponents.shape[2]
    tile_rows = min(128, local_rows)
    scales = jnp.exp2(exponents.astype(jnp.float32))
    q_real = q_vals.astype(jnp.float32) * expand(scales[0], scale_rows)
    k_real = k_vals.astype(jnp.float32) * expand(scales[1], scale_rows)
    v_real = v_vals.astype(jnp.float32) * expand(scales[2], scale_rows)
    gated_input = (k_real * v_real).astype(jnp.bfloat16)
    grad_mix = (q_real * grad_out.astype(jnp.float32)).astype(jnp.bfloat16)
    full_input, full_grad = (
        lax.all_to_all(gated_input, "ctx", split_axis=0, concat_axis=1, tiled=True),
        lax.all_to_all(grad_mix, "ctx", split_axis=0, concat_axis=1, tiled=True),
    )
    seq_len = full_input.shape[1]
    own_groups = full_input.shape[0] // group_width
    group_start = lax.axis_index("ctx") * own_groups
    own_taps = lax.dynamic_slice_in_dim(filter_taps, group_start, own_groups, 0)
    sources = jnp.concatenate([full_input[:, seq_len - filter_len :], full_input], axis=1)
    targets = jnp.concatenate([full_grad, full_grad[:, :filter_len]], axis=1)
    whole_w, whole_gz, lag_whole = convolve(sources, targets, full_grad, own_taps, tile_rows)
    conv_out, grad_z = (
        lax.all_to_all(whole_w, "ctx", split_axis=1, concat_axis=0, tiled=True),
        lax.all_to_all(whole_gz, "ctx", split_axis=1, concat_axis=0, tiled=True),
    )
    grad_filter = lax.all_to_all(lag_whole, "ctx", split_axis=1, concat_axis=0, tiled=True)
    grad_gate = grad_out.astype(jnp.float32) * conv_out
    grad_key = grad_z * v_real
    grad_value = grad_z * k_real

    def row_max(values):
        return jnp.max(
            jnp.abs(values).reshape(channels, local_rows // scale_rows, scale_rows), axis=(0, 2)
        )

    local_peak = jnp.stack([row_max(grad_gate), row_max(grad_key), row_max(grad_value)])
    block_peak = lax.pmax(local_peak, "ch")

    def scaled(values, peak_row):
        return (values / (jnp.repeat(peak_row, scale_rows) + EPS)[None, :]).astype(jnp.bfloat16)

    return (
        scaled(grad_gate, block_peak[0]),
        scaled(grad_key, block_peak[1]),
        scaled(grad_value, block_peak[2]),
        grad_filter,
        block_peak,
    )


def solution(mesh):
    in_specs = (
        P("ch", "ctx"),
        P("ch", "ctx"),
        P("ch", "ctx"),
        P("ch", "ctx"),
        P(None, "ch", "ctx"),
        P("ch", None),
    )
    out_specs = (P("ch", "ctx"), P("ch", "ctx"), P("ch", "ctx"), P("ch", "ctx"), P(None, "ctx"))
    return jax.shard_map(shards, mesh=mesh, in_specs=in_specs, out_specs=out_specs, check_vma=False)
```

profile of v0, /device:TPU:0, one launch (start us, length us, event | category | flops | bytes accessed | tf_op | source)
XLA Modules:
  0.0 368.7 jit_solution(3180230721884915900)
XLA Ops:
  1.6 4.7 %broadcast_in_dim.58 = f32[2048,2,128]{2,1,0:T(2,128)S(1)} broadcast(f32[2048,2]{1,0:T(8,128)S(1)} %bitcast.154), dimensions={0,1} | broadcast | bytes 2113536 | tf_op jit(solution)/shard_map/broadcast_in_dim | solution.py:10
  7.6 5.2 %all-to-all-start.1 = ((bf16[8,256,256]{2,1,0:T(8,128)(2,1)}), bf16[8,256,256]{2,1,0:T(8,128)(2,1)S(1)}, u32[]{:S(2)}, u32[]{:S(2)}) async-start(bf16[8,256,256]{2,1,0:T(8,128)(2,1)} %bitcast.9), calls=%async_computation.1 | async-start | bytes 2097152 | tf_op jit(solution)/shard_map/all_to_all | solution.py:85
  13.0 4.7 %broadcast_in_dim.54 = f32[2048,2,128]{2,1,0:T(2,128)S(1)} broadcast(f32[2048,2]{1,0:T(8,128)S(1)} %bitcast.155), dimensions={0,1} | broadcast | bytes 2113536 | tf_op jit(solution)/shard_map/broadcast_in_dim | solution.py:10
  17.8 4.7 %broadcast_in_dim.56 = f32[2048,2,128]{2,1,0:T(2,128)S(1)} broadcast(f32[2048,2]{1,0:T(8,128)S(1)} %bitcast.156), dimensions={0,1} | broadcast | bytes 2113536 | tf_op jit(solution)/shard_map/broadcast_in_dim | solution.py:10
  28.2 4.4 %all-to-all-start = ((bf16[8,256,256]{2,1,0:T(8,128)(2,1)}), bf16[8,256,256]{2,1,0:T(8,128)(2,1)}, u32[]{:S(2)}, u32[]{:S(2)}) async-start(bf16[8,256,256]{2,1,0:T(8,128)(2,1)} %bitcast.4), calls=%async_computation | async-start | bytes 2097152 | tf_op jit(solution)/shard_map/all_to_all | solution.py:84
  34.8 13.1 %all-to-all-done = bf16[8,256,256]{2,1,0:T(8,128)(2,1)} async-done(((bf16[8,256,256]{2,1,0:T(8,128)(2,1)}), bf16[8,256,256]{2,1,0:T(8,128)(2,1)}, u32[]{:S(2)}, u32[]{:S(2)}) %all-to-all-start) | async-done | bytes 1048608 | tf_op jit(solution)/shard_map/all_to_all | solution.py:84
  61.9 211.8 %while.20 = (s32[]{:T(128)}, f32[16,16,16,128]{3,2,1,0:T(8,128)}, f32[16,16,16,128]{3,2,1,0:T(8,128)}, f32[16,1280]{1,0:T(8,128)S(1)}, bf16[16,16,24,128]{3,2,1,...) while((s32[]{:T(128)}, f32[16,16,16,128]{3,2,1,0:T(8,128)}, ...), condition=%wide.region_2.3_spmd.clone, body=%wide.region_0.2_spmd.clone.sunk | while | flops 405288960 | bytes 44138964 | solution.py:63
  67.7 4.8 %reshape.152 = f32[16,128,255]{2,1,0:T(8,128)S(1)} reshape(f32[16,32640]{1,0:T(8,128)} %slice.129) | data formatting | bytes 4177920 | tf_op jit(solution)/shard_map/while/body/eval_jaxpr/reshape | solution.py:52
  90.0 4.8 %reshape.152 = f32[16,128,255]{2,1,0:T(8,128)S(1)} reshape(f32[16,32640]{1,0:T(8,128)} %slice.129) | data formatting | bytes 4177920 | tf_op jit(solution)/shard_map/while/body/eval_jaxpr/reshape | solution.py:52
  103.8 3.9 %select_add_fusion.4 = f32[16,16,16,128]{3,2,1,0:T(8,128)} fusion(f32[16,16,16,128]{3,2,1,0:T(8,128)} %get-tuple-element.366, pred[]{:T(512)S(6)} %compare.5, bf16[16,16,24,128]{3,2,1,0:T(8,128)(2,1)} %get-tuple-element.386, s32[]{:T(128)S(6)} %select_n.49, bf16[16,128,255]{2,1,0:T(8,128)(2,1)S(1)} %reshape.151), kind=kOutput, calls=%fused_computation.1.clone.1 | convolution fusion | flops 135266304 | bytes 5767173 | tf_op jit(solution)/shard_map/while/body/eval_jaxpr/gij,gcpj->gcpi/dot_general | solution.py:41
  113.7 4.8 %reshape.152 = f32[16,128,255]{2,1,0:T(8,128)S(1)} reshape(f32[16,32640]{1,0:T(8,128)} %slice.129) | data formatting | bytes 4177920 | tf_op jit(solution)/shard_map/while/body/eval_jaxpr/reshape | solution.py:52
  137.5 4.8 %reshape.152 = f32[16,128,255]{2,1,0:T(8,128)S(1)} reshape(f32[16,32640]{1,0:T(8,128)} %slice.129) | data formatting | bytes 4177920 | tf_op jit(solution)/shard_map/while/body/eval_jaxpr/reshape | solution.py:52
  151.3 3.9 %select_add_fusion.4 = f32[16,16,16,128]{3,2,1,0:T(8,128)} fusion(f32[16,16,16,128]{3,2,1,0:T(8,128)} %get-tuple-element.366, pred[]{:T(512)S(6)} %compare.5, bf16[16,16,24,128]{3,2,1,0:T(8,128)(2,1)} %get-tuple-element.386, s32[]{:T(128)S(6)} %select_n.49, bf16[16,128,255]{2,1,0:T(8,128)(2,1)S(1)} %reshape.151), kind=kOutput, calls=%fused_computation.1.clone.1 | convolution fusion | flops 135266304 | bytes 5767173 | tf_op jit(solution)/shard_map/while/body/eval_jaxpr/gij,gcpj->gcpi/dot_general | solution.py:41
  161.2 4.8 %reshape.152 = f32[16,128,255]{2,1,0:T(8,128)S(1)} reshape(f32[16,32640]{1,0:T(8,128)} %slice.129) | data formatting | bytes 4177920 | tf_op jit(solution)/shard_map/while/body/eval_jaxpr/reshape | solution.py:52
  185.0 4.8 %reshape.152 = f32[16,128,255]{2,1,0:T(8,128)S(1)} reshape(f32[16,32640]{1,0:T(8,128)} %slice.129) | data formatting | bytes 4177920 | tf_op jit(solution)/shard_map/while/body/eval_jaxpr/reshape | solution.py:52
  208.7 4.8 %reshape.152 = f32[16,128,255]{2,1,0:T(8,128)S(1)} reshape(f32[16,32640]{1,0:T(8,128)} %slice.129) | data formatting | bytes 4177920 | tf_op jit(solution)/shard_map/while/body/eval_jaxpr/reshape | solution.py:52
  232.5 4.8 %reshape.152 = f32[16,128,255]{2,1,0:T(8,128)S(1)} reshape(f32[16,32640]{1,0:T(8,128)} %slice.129) | data formatting | bytes 4177920 | tf_op jit(solution)/shard_map/while/body/eval_jaxpr/reshape | solution.py:52
  256.2 4.8 %reshape.152 = f32[16,128,255]{2,1,0:T(8,128)S(1)} reshape(f32[16,32640]{1,0:T(8,128)} %slice.129) | data formatting | bytes 4177920 | tf_op jit(solution)/shard_map/while/body/eval_jaxpr/reshape | solution.py:52
  277.6 4.5 %all-to-all-start.2 = ((f32[256,8,256]{2,0,1:T(8,128)}), f32[256,8,256]{2,0,1:T(8,128)}, u32[]{:S(2)}, u32[]{:S(2)}) async-start(f32[256,8,256]{2,0,1:T(8,128)} %copy.52), calls=%async_computation.2 | async-start | bytes 4194304 | tf_op jit(solution)/shard_map/all_to_all | solution.py:95
  287.3 21.4 %all-to-all-done.2 = f32[256,8,256]{2,0,1:T(8,128)} async-done(((f32[256,8,256]{2,0,1:T(8,128)}), f32[256,8,256]{2,0,1:T(8,128)}, u32[]{:S(2)}, u32[]{:S(2)}) %all-to-all-start.2) | async-done | bytes 2097184 | tf_op jit(solution)/shard_map/all_to_all | solution.py:95
  308.7 4.4 %all-to-all-start.3 = ((f32[256,8,256]{2,0,1:T(8,128)}), f32[256,8,256]{2,0,1:T(8,128)}, u32[]{:S(2)}, u32[]{:S(2)}) async-start(f32[256,8,256]{2,0,1:T(8,128)} %copy.53), calls=%async_computation.3 | async-start | bytes 4194304 | tf_op jit(solution)/shard_map/all_to_all | solution.py:96
  315.9 23.8 %all-to-all-done.3 = f32[256,8,256]{2,0,1:T(8,128)} async-done(((f32[256,8,256]{2,0,1:T(8,128)}), f32[256,8,256]{2,0,1:T(8,128)}, u32[]{:S(2)}, u32[]{:S(2)}) %all-to-all-start.3) | async-done | bytes 2097184 | tf_op jit(solution)/shard_map/all_to_all | solution.py:96
  348.0 11.9 %pmax.7 = f32[3,2]{1,0:T(4,128)S(1)} all-reduce(f32[3,2]{1,0:T(4,128)S(1)} %pad_maximum_fusion.3), channel_id=1, replica_groups=mesh['ctx'=8,'ch'=4] {'ch'}, use_global_device_ids=true, to_apply=%region_9.10 | all-reduce | flops 6 | bytes 48 | tf_op jit(solution)/shard_map/pmax | solution.py:109
  364.1 3.9 %divide_convert_fusion = (bf16[2048,256]{1,0:T(8,128)(2,1)}, bf16[2048,256]{1,0:T(8,128)(2,1)}) fusion(f32[256]{0:T(256)S(1)} %broadcast_bitcast_fusion, f32[256,8,2,128]{3,2,1,0:T(2,128)S(1)} %bitcast.140, bf16[2048,256]{1,0:T(8,128)(2,1)S(1)} %copy-done.9, f32[256,8,256]{2,0,1:T(8,128)} %all-to-all-done.3, f32[256]{0:T(256)S(1)} %broadcast_bitcast_fusion.1, ...), kind=kLoop, calls=%fused_computation.22 | loop fusion | flops 5242880 | bytes 10487808 | tf_op jit(solution)/shard_map/convert_element_type | solution.py:112
  (244 shorter events, 209.1 us)
Async XLA Ops:
  0.6 32.0 %copy-start = (f32[128,1024]{1,0:T(8,128)S(1)}, f32[128,1024]{1,0:T(8,128)}, u32[]{:S(2)}) copy-start(f32[128,1024]{1,0:T(8,128)} %param.13) | copy-start | bytes 1572868
  1.5 4.8 %copy-start.7 = (bf16[2048,256]{1,0:T(8,128)(2,1)S(1)}, bf16[2048,256]{1,0:T(8,128)(2,1)}, u32[]{:S(2)}) copy-start(bf16[2048,256]{1,0:T(8,128)(2,1)} %param.11) | copy-start | bytes 3145732
  1.5 4.8 %copy-start.13 = (bf16[2048,256]{1,0:T(8,128)(2,1)S(1)}, bf16[2048,256]{1,0:T(8,128)(2,1)}, u32[]{:S(2)}) copy-start(bf16[2048,256]{1,0:T(8,128)(2,1)} %param.8) | copy-start | bytes 3145732
  7.6 20.6 %all-to-all-start.1 = ((bf16[8,256,256]{2,1,0:T(8,128)(2,1)}), bf16[8,256,256]{2,1,0:T(8,128)(2,1)S(1)}, u32[]{:S(2)}, u32[]{:S(2)}) async-start(bf16[8,256,256]{2,1,0:T(8,128)(2,1)} %bitcast.9), calls=%async_computation.1 | async-start | bytes 2097152 | tf_op jit(solution)/shard_map/all_to_all | solution.py:85
  17.7 4.8 %copy-start.3 = (f32[2048,2,128]{2,1,0:T(2,128)}, f32[2048,2,128]{2,1,0:T(2,128)S(1)}, u32[]{:S(2)}) copy-start(f32[2048,2,128]{2,1,0:T(2,128)S(1)} %broadcast_in_dim.54) | copy-start | bytes 6291460
  17.7 6.1 %copy-start.8 = (bf16[2048,256]{1,0:T(8,128)(2,1)S(1)}, bf16[2048,256]{1,0:T(8,128)(2,1)}, u32[]{:S(2)}) copy-start(bf16[2048,256]{1,0:T(8,128)(2,1)} %param.9) | copy-start | bytes 3145732
  17.7 6.1 %copy-start.10 = (bf16[2048,256]{1,0:T(8,128)(2,1)S(1)}, bf16[2048,256]{1,0:T(8,128)(2,1)}, u32[]{:S(2)}) copy-start(bf16[2048,256]{1,0:T(8,128)(2,1)} %param.10) | copy-start | bytes 3145732
  22.5 1.3 copy-start.5
  28.2 19.7 %all-to-all-start = ((bf16[8,256,256]{2,1,0:T(8,128)(2,1)}), bf16[8,256,256]{2,1,0:T(8,128)(2,1)}, u32[]{:S(2)}, u32[]{:S(2)}) async-start(bf16[8,256,256]{2,1,0:T(8,128)(2,1)} %bitcast.4), calls=%async_computation | async-start | bytes 2097152 | tf_op jit(solution)/shard_map/all_to_all | solution.py:84
  59.2 1.5 copy-start.12
  277.6 4.5 %copy-start.2 = (f32[16,16,16,128]{3,2,1,0:T(8,128)S(1)}, f32[16,16,16,128]{3,2,1,0:T(8,128)}, u32[]{:S(2)}) copy-start(f32[16,16,16,128]{3,2,1,0:T(8,128)} %get-tuple-element.208) | copy-start | bytes 6291460
  277.6 31.1 %all-to-all-start.2 = ((f32[256,8,256]{2,0,1:T(8,128)}), f32[256,8,256]{2,0,1:T(8,128)}, u32[]{:S(2)}, u32[]{:S(2)}) async-start(f32[256,8,256]{2,0,1:T(8,128)} %copy.52), calls=%async_computation.2 | async-start | bytes 4194304 | tf_op jit(solution)/shard_map/all_to_all | solution.py:95
  308.7 31.0 %all-to-all-start.3 = ((f32[256,8,256]{2,0,1:T(8,128)}), f32[256,8,256]{2,0,1:T(8,128)}, u32[]{:S(2)}, u32[]{:S(2)}) async-start(f32[256,8,256]{2,0,1:T(8,128)} %copy.53), calls=%async_computation.3 | async-start | bytes 4194304 | tf_op jit(solution)/shard_map/all_to_all | solution.py:96
  313.1 30.0 %copy-start.4 = (f32[2048,2,128]{2,1,0:T(2,128)S(1)}, f32[2048,2,128]{2,1,0:T(2,128)}, u32[]{:S(2)}) copy-start(f32[2048,2,128]{2,1,0:T(2,128)} %copy-done.3) | copy-start | bytes 6291460
  339.7 8.3 %all-to-all-start.4 = ((f32[16,8,128]{2,0,1:T(8,128)}), f32[16,8,128]{2,0,1:T(8,128)S(1)}, u32[]{:S(2)}, u32[]{:S(2)}) async-start(f32[16,8,128]{2,0,1:T(8,128)} %copy_bitcast_fusion), calls=%async_computation.4 | async-start | bytes 131072 | tf_op jit(solution)/shard_map/all_to_all | solution.py:98
  360.8 3.3 copy-start.6
  360.8 3.3 copy-start.9
  360.8 3.3 copy-start.11
  364.1 4.6 %copy-start.1 = (f32[128,1024]{1,0:T(8,128)S(1)}, f32[128,1024]{1,0:T(8,128)}, u32[]{:S(2)}) copy-start(f32[128,1024]{1,0:T(8,128)} %param.13) | copy-start | bytes 1572868
where the time goes:
time: 370 us; the launch traced here: 369 us
  local copies, waits for them, and re-layouts  160 us (43%)
  matrix products  89.4 us (24%)
  waiting for transfers between devices  62.7 us (17%)
  starting transfers between devices  21.8 us (6%)
  other arithmetic  21.2 us (6%)
  blocking collectives  11.9 us (3%)
    reshape x9, local copies, waits for them, and re-layouts, one_offset(): diagonal = jnp.sum(skewed.reshape(groups, tile_rows, diag_len), axis=1)  43.3 us
    dot_general x9, matrix products, one_offset(): jnp.einsum('gij,gcpj->gcpi', toeplitz, z_src, preferred_element_type=jnp....  34.6 us
    dot_general x9, matrix products, one_offset(): jnp.einsum('gji,gcpj->gcpi', toeplitz, g_src, preferred_element_type=jnp....  34.5 us
    reshape x9, local copies, waits for them, and re-layouts, toeplitz_tile(): return flat.reshape(groups, tile_rows, 2 * tile_rows - 1)[:, :, :tile_rows]  30.2 us
    all_to_all x1, waiting for transfers between devices, shards(): lax.all_to_all(whole_gz, 'ctx', split_axis=1, concat_axis=0, tiled=True)  23.8 us
    all_to_all x1, waiting for transfers between devices, shards(): lax.all_to_all(whole_w, 'ctx', split_axis=1, concat_axis=0, tiled=True)  21.4 us
    dot_general x9, matrix products, one_offset(): jnp.einsum('gcpi,gcpj->gij', local_grad, z_src, preferred_element_type=jn...  20.3 us
    while x27, local copies, waits for them, and re-layouts  19.2 us
  transfers between devices with their start and end apart: 5, of which 5 were waited for; matrix products, arithmetic and copies ran while one was open for 6% of the time, Pallas kernels for 0%

commit v1 on v0

v1 whole, which is shorter than its diff:
```python
import functools

import jax
import jax.numpy as jnp
from jax import lax
from jax.experimental import pallas as pl
from jax.experimental.pallas import tpu as pltpu
from jax.sharding import PartitionSpec as P

EPS = 1e-06
MESH = pl.DeviceIdType.MESH
CHUNKS = 4
HALF = 128


def exchange_kernel(
    n, m, group_width, scale_rows, blocks,
    q_ref, k_ref, v_ref, g_ref, sc_ref, taps_ref,
    conv_out, filt_out, peak_out,
    zs, zf, ws, wr, tt, gfs, gfr, peak, pks,
    in_send, in_recv, back_send, back_recv, out_sem, gf_send, gf_recv, pk_send, pk_recv,
):
    me = lax.axis_index("ctx")
    row_me = lax.axis_index("ch")
    channels, rows = q_ref.shape
    own = channels // n
    chunk = own // CHUNKS
    own_groups = own // group_width
    chunk_groups = own_groups // CHUNKS
    scale_blocks = channels // scale_rows
    filter_len = taps_ref.shape[1]
    lead = filter_len // rows
    cols = filter_len // n
    width = filter_len + HALF
    f32 = jnp.float32

    barrier = pltpu.get_barrier_semaphore()

    def greet_ctx(i, c):
        pl.semaphore_signal(
            barrier, inc=1, device_id={"ctx": lax.rem(me + i, n)}, device_id_type=MESH
        )
        return c

    def greet_ch(i, c):
        pl.semaphore_signal(
            barrier, inc=1, device_id={"ch": lax.rem(row_me + i, m)}, device_id_type=MESH
        )
        return c

    lax.fori_loop(1, n, greet_ctx, 0)
    lax.fori_loop(1, m, greet_ch, 0)

    def at_rows(owner, j):
        return pl.ds(pl.multiple_of(owner * own + j * chunk, 16), chunk)

    def scale_of(which, owner, j):
        return sc_ref[which * scale_blocks + (owner * own + j * chunk) // scale_rows]

    def real(ref, which, owner, j):
        return ref[at_rows(owner, j), :].astype(f32) * scale_of(which, owner, j)

    def mixed(owner, j):
        z = (real(k_ref, 1, owner, j) * real(v_ref, 2, owner, j)).astype(jnp.bfloat16)
        gw = (real(q_ref, 0, owner, j) * g_ref[at_rows(owner, j), :].astype(f32)).astype(jnp.bfloat16)
        return z, gw

    def in_copy(j, dst, src):
        return pltpu.make_async_remote_copy(
            src_ref=zs.at[:, at_rows(dst, j), :],
            dst_ref=zf.at[src, :, pl.ds(pl.multiple_of(j * chunk, 16), chunk), :],
            send_sem=in_send.at[j, dst],
            recv_sem=in_recv.at[j, src],
            device_id={"ctx": dst},
            device_id_type=MESH,
        )

    def back_copy(j, dst, src):
        return pltpu.make_async_remote_copy(
            src_ref=ws.at[dst, :, pl.ds(pl.multiple_of(j * chunk, 16), chunk), :],
            dst_ref=wr.at[:, at_rows(src, j), :],
            send_sem=back_send.at[j, dst],
            recv_sem=back_recv.at[j, src],
            device_id={"ctx": dst},
            device_id_type=MESH,
        )

    def gf_copy(dst, src):
        return pltpu.make_async_remote_copy(
            src_ref=gfs.at[dst],
            dst_ref=gfr.at[src],
            send_sem=gf_send.at[dst],
            recv_sem=gf_recv.at[src],
            device_id={"ctx": dst},
            device_id_type=MESH,
        )

    def pk_copy(dst, src):
        return pltpu.make_async_remote_copy(
            src_ref=pks.at[row_me],
            dst_ref=pks.at[src],
            send_sem=pk_send.at[dst],
            recv_sem=pk_recv.at[src],
            device_id={"ch": dst},
            device_id_type=MESH,
        )

    def out_copy(j, owner):
        return pltpu.make_async_copy(
            wr.at[:, at_rows(owner, j), :], conv_out.at[:, at_rows(owner, j), :], out_sem.at[j, owner]
        )

    pl.semaphore_wait(barrier, n - 1 + m - 1)

    def send_chunk(j, c):
        def one(i, c):
            dst = lax.rem(me + i, n)
            z, gw = mixed(dst, j)
            zs[0, at_rows(dst, j), :] = z
            zs[1, at_rows(dst, j), :] = gw
            in_copy(j, dst, me).start()
            return c

        lax.fori_loop(1, n, one, 0)
        z, gw = mixed(me, j)
        here = pl.ds(pl.multiple_of(j * chunk, 16), chunk)
        zf[me, 0, here, :] = z
        zf[me, 1, here, :] = gw
        return c

    lax.fori_loop(0, CHUNKS, send_chunk, 0)

    peak[...] = jnp.zeros_like(peak)
    flip = (
        lax.broadcasted_iota(jnp.int32, (HALF, HALF), 0)
        + lax.broadcasted_iota(jnp.int32, (HALF, HALF), 1)
        == HALF - 1
    ).astype(f32).astype(jnp.bfloat16)
    zero = jnp.zeros((HALF, HALF), jnp.bfloat16)

    def turned(x, by):
        by = (by * group_width) % x.shape[0]
        return x if by == 0 else jnp.concatenate([x[-by:], x[:-by]], axis=0)

    def one_group(gi, c):
        at = pl.ds(pl.multiple_of(gi * group_width, 16), group_width)
        z = zf[:, 0, at, :].reshape(n * group_width, rows)
        gw = zf[:, 1, at, :].reshape(n * group_width, rows)
        taps = taps_ref[pl.ds(me * own_groups + gi, 1), :].astype(jnp.bfloat16).astype(f32)
        line = jnp.concatenate([taps, jnp.zeros((1, HALF), f32)], axis=1)
        band = pltpu.roll(
            jnp.broadcast_to(line, (HALF, width)), 0, 1, stride=1, stride_axis=0
        ).astype(jnp.bfloat16)

        def tile(i):
            if i < 0 or i * HALF >= width:
                return zero
            return band[:, i * HALF : (i + 1) * HALF]

        per = rows // HALF
        for o in range(lead + 1):
            for a in range(per):
                for b in range(per):
                    tt[o * rows + a * HALF : o * rows + (a + 1) * HALF, b * HALF : (b + 1) * HALF] = tile(
                        o * per + b - a
                    )
        zwin = jnp.concatenate([turned(z, o) for o in range(lead + 1)], axis=1)
        w = jnp.dot(zwin, tt[...], preferred_element_type=f32)
        gparts = [turned(gw, -o) for o in range(lead + 1)]
        gz = jnp.zeros((n * group_width, rows), f32)
        for o in range(lead + 1):
            gz = gz + lax.dot_general(
                gparts[o], tt[o * rows : (o + 1) * rows, :], (((1,), (1,)), ((), ())),
                preferred_element_type=f32,
            )
        ws[:, 0, at, :] = w.astype(jnp.bfloat16).reshape(n, group_width, rows)
        ws[:, 1, at, :] = gz.astype(jnp.bfloat16).reshape(n, group_width, rows)

        gwin = jnp.concatenate(gparts, axis=1)
        zcat = jnp.concatenate([z[:, a * HALF : (a + 1) * HALF] for a in range(per)], axis=0)
        gcat = jnp.concatenate([gwin[:, a * HALF : a * HALF + width] for a in range(per)], axis=0)
        zrev = lax.dot_general(
            flip, zcat, (((1,), (1,)), ((), ())), preferred_element_type=f32
        ).astype(jnp.bfloat16)
        cross = jnp.dot(zrev, gcat, preferred_element_type=f32)
        skewed = pltpu.roll(cross, width - (HALF - 1), 1, stride=1, stride_axis=0)
        lags = jnp.sum(skewed, axis=0, keepdims=True)
        for d in range(n):
            gfs[d, pl.ds(gi, 1), :] = lags[:, d * cols : (d + 1) * cols]
        return c

    def note_peak(j, owner):
        conv = wr[0, at_rows(owner, j), :].astype(f32)
        gz = wr[1, at_rows(owner, j), :].astype(f32)
        gq = g_ref[at_rows(owner, j), :].astype(f32) * conv
        gk = gz * real(v_ref, 2, owner, j)
        gv = gz * real(k_ref, 1, owner, j)
        for i, x in enumerate((gq, gk, gv)):
            peak[i] = jnp.maximum(peak[i], jnp.max(jnp.abs(x).reshape(chunk // 8, 8, rows), axis=0))

    def take_back(j):
        def one(i, c):
            src = lax.rem(me + n - i, n)
            back_copy(j, me, src).wait_recv()
            out_copy(j, src).start()
            note_peak(j, src)
            return c

        lax.fori_loop(1, n, one, 0)
        out_copy(j, me).start()
        note_peak(j, me)

    def work_chunk(j, c):
        def arrive(i, c):
            src = lax.rem(me + n - i, n)
            in_copy(j, me, src).wait_recv()
            return c

        lax.fori_loop(1, n, arrive, 0)
        lax.fori_loop(j * chunk_groups, (j + 1) * chunk_groups, one_group, 0)

        def reply(i, c):
            back_copy(j, lax.rem(me + i, n), me).start()
            return c

        lax.fori_loop(1, n, reply, 0)
        here = pl.ds(pl.multiple_of(j * chunk, 16), chunk)
        for i in range(2):
            wr[i, at_rows(me, j), :] = ws[me, i, here, :]
        return c

    lax.fori_loop(0, CHUNKS, work_chunk, 0)

    def send_gf(i, c):
        gf_copy(lax.rem(me + i, n), me).start()
        return c

    lax.fori_loop(1, n, send_gf, 0)

    def take_chunk(j, c):
        take_back(j)
        return c

    lax.fori_loop(0, CHUNKS, take_chunk, 0)

    for i in range(3):
        lanes = jnp.max(peak[i], axis=0, keepdims=True)
        per = rows // blocks
        pks[row_me, i : i + 1, :] = jnp.concatenate(
            [
                jnp.broadcast_to(jnp.max(lanes[:, b * per : (b + 1) * per], axis=1, keepdims=True), (1, per))
                for b in range(blocks)
            ],
            axis=1,
        )
    pks[row_me, 3:8, :] = jnp.zeros((5, rows), f32)

    def send_pk(i, c):
        pk_copy(lax.rem(row_me + i, m), row_me).start()
        return c

    lax.fori_loop(1, m, send_pk, 0)

    gfr[me] = gfs[me]

    def settle_ctx(i, c):
        dst = lax.rem(me + i, n)
        src = lax.rem(me + n - i, n)
        gf_copy(me, src).wait_recv()
        gf_copy(dst, me).wait_send()

        def both(j, c):
            in_copy(j, dst, me).wait_send()
            back_copy(j, dst, me).wait_send()
            return c

        lax.fori_loop(0, CHUNKS, both, 0)
        return c

    lax.fori_loop(1, n, settle_ctx, 0)
    filt_out[...] = gfr[...]

    def settle_ch(i, c):
        pk_copy(row_me, lax.rem(row_me + m - i, m)).wait_recv()
        pk_copy(lax.rem(row_me + i, m), row_me).wait_send()
        return c

    lax.fori_loop(1, m, settle_ch, 0)
    peak_out[...] = jnp.max(pks[...], axis=0)

    def settle_out(j, c):
        def one(i, c):
            out_copy(j, i).wait()
            return c

        lax.fori_loop(0, n, one, 0)
        return c

    lax.fori_loop(0, CHUNKS, settle_out, 0)


def scale_kernel(scale_rows, conv_ref, g_ref, k_ref, v_ref, sc_ref, peak_ref, oq, ok, ov):
    f32 = jnp.float32
    inv = 1.0 / (peak_ref[0:3, :] + EPS)
    conv = conv_ref[0].astype(f32)
    gz = conv_ref[1].astype(f32)
    oq[...] = (g_ref[...].astype(f32) * conv * inv[0:1]).astype(jnp.bfloat16)
    for b in range(g_ref.shape[0] // scale_rows):
        at = slice(b * scale_rows, (b + 1) * scale_rows)
        part = gz[at]
        ok[at, :] = (part * (v_ref[at, :].astype(f32) * sc_ref[1, b]) * inv[1:2]).astype(jnp.bfloat16)
        ov[at, :] = (part * (k_ref[at, :].astype(f32) * sc_ref[0, b]) * inv[2:3]).astype(jnp.bfloat16)


def shards(n, m, q_vals, k_vals, v_vals, grad_out, exponents, filter_taps):
    channels, rows = q_vals.shape
    groups, filter_len = filter_taps.shape
    _, scale_blocks, blocks = exponents.shape
    scale_rows = channels // scale_blocks
    group_width = channels // groups
    own = channels // n
    own_groups = groups // n
    cols = filter_len // n
    lead = filter_len // rows
    bf16, f32 = jnp.bfloat16, jnp.float32
    scales = jnp.repeat(jnp.exp2(exponents.astype(f32)), rows // blocks, axis=2)
    vmem = pl.BlockSpec(memory_space=pltpu.VMEM)
    dma = pltpu.SemaphoreType.DMA
    conv, filt, peak = pl.pallas_call(
        functools.partial(exchange_kernel, n, m, group_width, scale_rows, blocks),
        out_shape=(
            jax.ShapeDtypeStruct((2, channels, rows), bf16),
            jax.ShapeDtypeStruct((n, own_groups, cols), f32),
            jax.ShapeDtypeStruct((8, rows), f32),
        ),
        in_specs=[vmem] * 6,
        out_specs=(pl.BlockSpec(memory_space=pl.ANY), vmem, vmem),
        scratch_shapes=[
            pltpu.VMEM((2, channels, rows), bf16),
            pltpu.VMEM((n, 2, own, rows), bf16),
            pltpu.VMEM((n, 2, own, rows), bf16),
            pltpu.VMEM((2, channels, rows), bf16),
            pltpu.VMEM(((lead + 1) * rows, rows), bf16),
            pltpu.VMEM((n, own_groups, cols), f32),
            pltpu.VMEM((n, own_groups, cols), f32),
            pltpu.VMEM((3, 8, rows), f32),
            pltpu.VMEM((m, 8, rows), f32),
            dma((CHUNKS, n)),
            dma((CHUNKS, n)),
            dma((CHUNKS, n)),
            dma((CHUNKS, n)),
            dma((CHUNKS, n)),
            dma((n,)),
            dma((n,)),
            dma((m,)),
            dma((m,)),
        ],
        compiler_params=pltpu.CompilerParams(
            collective_id=0, has_side_effects=True, vmem_limit_bytes=48 * 1024 * 1024
        ),
    )(
        q_vals, k_vals, v_vals, grad_out,
        scales.reshape(3 * scale_blocks, 1, rows), filter_taps,
    )
    tile = min(256, channels)
    flat = pl.BlockSpec((tile, rows), lambda i: (i, 0))
    grads = pl.pallas_call(
        functools.partial(scale_kernel, scale_rows),
        grid=(channels // tile,),
        out_shape=tuple(jax.ShapeDtypeStruct((channels, rows), bf16) for _ in range(3)),
        in_specs=[
            pl.BlockSpec((2, tile, rows), lambda i: (0, i, 0)),
            flat, flat, flat,
            pl.BlockSpec((2, tile // scale_rows, 1, rows), lambda i: (0, i, 0, 0)),
            pl.BlockSpec((8, rows), lambda i: (0, 0)),
        ],
        out_specs=(flat, flat, flat),
    )(conv, grad_out, k_vals, v_vals, scales[1:3].reshape(2, scale_blocks, 1, rows), peak)
    return (*grads, filt.reshape(groups, cols), peak[0:3, :: rows // blocks])


def solution(mesh):
    in_specs = (
        P("ch", "ctx"),
        P("ch", "ctx"),
        P("ch", "ctx"),
        P("ch", "ctx"),
        P(None, "ch", "ctx"),
        P("ch", None),
    )
    out_specs = (P("ch", "ctx"), P("ch", "ctx"), P("ch", "ctx"), P("ch", "ctx"), P(None, "ctx"))
    body = functools.partial(shards, mesh.shape["ctx"], mesh.shape["ch"])
    return jax.shard_map(body, mesh=mesh, in_specs=in_specs, out_specs=out_specs, check_vma=False)
```

time: 370 us -> 75.3 us (0.20)
  local copies, waits for them, and re-layouts: 160 us -> 9.6 us
  matrix products: 89.4 us -> 0 us
  Pallas kernels: 0 us -> 63.8 us
  waiting for transfers between devices: 62.7 us -> 0 us
  starting transfers between devices: 21.8 us -> 0 us
  other arithmetic: 21.2 us -> 0.69 us
  blocking collectives: 11.9 us -> 0 us
    dot_general x27 -> x0, matrix products: 89.4 us -> none  [the longest x9 34.6 us: one_offset(): jnp.einsum('gij,gcpj->gcpi', toeplitz, z_src, preferred_element_type=jnp....]
    reshape x19 -> x0, local copies, waits for them, and re-layouts: 74.7 us -> none  [the longest x9 43.3 us: one_offset(): diagonal = jnp.sum(skewed.reshape(groups, tile_rows, diag_len), axis=1)]
    pallas_call x0 -> x2, Pallas kernels: none -> 63.8 us  [the longest x1 57.2 us: shards(): pl.pallas_call(functools.partial(exchange_kernel, n, m, group_width, scal...]
    all_to_all x5 -> x0, waiting for transfers between devices: 62.7 us -> none  [the longest x1 23.8 us: shards(): lax.all_to_all(whole_gz, 'ctx', split_axis=1, concat_axis=0, tiled=True)]
    all_to_all x5 -> x0, starting transfers between devices: 21.8 us -> none  [the longest x1 5.17 us: shards(): lax.all_to_all(grad_mix, 'ctx', split_axis=0, concat_axis=1, tiled=True)]
    while x27 -> x0, local copies, waits for them, and re-layouts: 19.2 us -> none
    slice x47 -> x3, local copies, waits for them, and re-layouts: 17.1 us -> 0.87 us  [the longest x1 0.78 us: shards(): return (*grads, filt.reshape(groups, cols), peak[0:3, ::rows // blocks])]
    broadcast_in_dim x16 -> x2, local copies, waits for them, and re-layouts: 14.9 us -> 0.83 us  [shards(): scales = jnp.repeat(jnp.exp2(exponents.astype(f32)), rows // blocks, axis=2)]
  transfers between devices with their start and end apart: 5 -> 0, of which waited for: 5 -> 0; matrix products, arithmetic and copies ran while one was open for 6% -> 0% of each run, Pallas kernels for 0% -> 0%
where the time goes in v1:
time: 75.3 us; the launch traced here: 74.7 us
  Pallas kernels  63.8 us (85%)
  local copies, waits for them, and re-layouts  9.6 us (13%)
    pallas_call x1, Pallas kernels, shards(): pl.pallas_call(functools.partial(exchange_kernel, n, m, group_width, scal...  57.2 us
    unnamed x14, local copies, waits for them, and re-layouts  7.8 us
    pallas_call x1, Pallas kernels, shards(): pl.pallas_call(functools.partial(scale_kernel, scale_rows), grid=(channel...  6.58 us

profile of v1, /device:TPU:0, one launch (start us, length us, event | category | flops | bytes accessed | tf_op | source)
XLA Modules:
  0.0 74.7 jit_solution(12403847220220833773)
XLA Ops:
  0.6 0.7 multiply_exponential_fusion
  1.3 0.1 copy.11
  1.4 0.1 broadcast_in_dim.5
  1.5 0.0 copy-start
  1.6 1.2 %copy-done = bf16[2048,256]{1,0:T(8,128)(2,1)S(1)} copy-done((bf16[2048,256]{1,0:T(8,128)(2,1)S(1)}, bf16[2048,256]{1,0:T(8,128)(2,1)}, u32[]{:S(2)}) %copy-start) | copy-done | bytes 1048600
  2.8 0.0 copy-start.1
  2.8 1.2 %copy-done.1 = bf16[2048,256]{1,0:T(8,128)(2,1)S(1)} copy-done((bf16[2048,256]{1,0:T(8,128)(2,1)S(1)}, bf16[2048,256]{1,0:T(8,128)(2,1)}, u32[]{:S(2)}) %copy-start.1) | copy-done | bytes 1048600
  4.0 0.0 copy-start.2
  4.0 1.2 %copy-done.2 = bf16[2048,256]{1,0:T(8,128)(2,1)S(1)} copy-done((bf16[2048,256]{1,0:T(8,128)(2,1)S(1)}, bf16[2048,256]{1,0:T(8,128)(2,1)}, u32[]{:S(2)}) %copy-start.2) | copy-done | bytes 1048600
  5.2 0.0 copy-start.3
  5.2 1.2 %copy-done.3 = bf16[2048,256]{1,0:T(8,128)(2,1)S(1)} copy-done((bf16[2048,256]{1,0:T(8,128)(2,1)S(1)}, bf16[2048,256]{1,0:T(8,128)(2,1)}, u32[]{:S(2)}) %copy-start.3) | copy-done | bytes 1048600
  6.4 0.0 copy-start.4
  6.5 1.0 %copy-done.4 = f32[128,1024]{1,0:T(8,128)S(1)} copy-done((f32[128,1024]{1,0:T(8,128)S(1)}, f32[128,1024]{1,0:T(8,128)}, u32[]{:S(2)}) %copy-start.4) | copy-done | bytes 524312
  7.5 57.2 %shard_map.101 = (bf16[2,2048,256]{2,1,0:T(8,128)(2,1)}, f32[8,16,128]{2,1,0:T(8,128)S(1)}, f32[8,256]{1,0:T(8,128)S(1)}) custom-call(bf16[2048,256]{1,0:T(8,128)(2,1)S(1)} %copy-done.3, bf16[2048,256]{1,0:T(8,128)(2,1)S(1)} %copy-done, bf16[2048,256]{1,0:T(8,128)(2,1)S(1)} %copy-done.1, bf16[2048,256]{1,0:T(8,128)(2,1)S(1)} %copy-done.2, ...), custom_call_target="tpu_custom_call" | custom-call | tf_op jit(solution)/shard_map/pallas_call | solution.py:329
  64.7 0.0 copy-start.5
  64.7 0.6 copy-done.5
  65.3 0.1 copy.12
  65.4 0.7 broadcast_in_dim.6
  66.1 6.6 %shard_map.102 = (bf16[2048,256]{1,0:T(8,128)(2,1)}, bf16[2048,256]{1,0:T(8,128)(2,1)}, bf16[2048,256]{1,0:T(8,128)(2,1)}) custom-call(bf16[2,2048,256]{2,1,0:T(8,128)(2,1)} %get-tuple-element.11.conv_ref, bf16[2048,256]{1,0:T(8,128)(2,1)} %g_ref.3, bf16[2048,256]{1,0:T(8,128)(2,1)} %k_ref.3, bf16[2048,256]{1,0:T(8,128)(2,1)} %v_ref.3, ...), custom_call_target="tpu_custom_call" | custom-call | tf_op jit(solution)/shard_map/pallas_call | solution.py:367
  72.7 0.8 %slice.9 = f32[3,2]{1,0:T(4,128)S(1)} slice(f32[8,256]{1,0:T(8,128)} %copy-done.5), slice={[0:3:1], [0:256:128]} | slice | bytes 48 | tf_op jit(solution)/shard_map/slice | solution.py:379
  73.4 0.7 copy.13
  74.1 0.6 copy.15
  (1 shorter events, 0.0 us)
Async XLA Ops:
  1.5 1.2 %copy-start = (bf16[2048,256]{1,0:T(8,128)(2,1)S(1)}, bf16[2048,256]{1,0:T(8,128)(2,1)}, u32[]{:S(2)}) copy-start(bf16[2048,256]{1,0:T(8,128)(2,1)} %k_ref.3) | copy-start | bytes 3145732
  2.8 1.2 %copy-start.1 = (bf16[2048,256]{1,0:T(8,128)(2,1)S(1)}, bf16[2048,256]{1,0:T(8,128)(2,1)}, u32[]{:S(2)}) copy-start(bf16[2048,256]{1,0:T(8,128)(2,1)} %v_ref.3) | copy-start | bytes 3145732
  4.0 1.2 %copy-start.2 = (bf16[2048,256]{1,0:T(8,128)(2,1)S(1)}, bf16[2048,256]{1,0:T(8,128)(2,1)}, u32[]{:S(2)}) copy-start(bf16[2048,256]{1,0:T(8,128)(2,1)} %g_ref.3) | copy-start | bytes 3145732
  5.2 1.2 %copy-start.3 = (bf16[2048,256]{1,0:T(8,128)(2,1)S(1)}, bf16[2048,256]{1,0:T(8,128)(2,1)}, u32[]{:S(2)}) copy-start(bf16[2048,256]{1,0:T(8,128)(2,1)} %q_ref.1) | copy-start | bytes 3145732
  6.4 1.0 %copy-start.4 = (f32[128,1024]{1,0:T(8,128)S(1)}, f32[128,1024]{1,0:T(8,128)}, u32[]{:S(2)}) copy-start(f32[128,1024]{1,0:T(8,128)} %taps_ref.1) | copy-start | bytes 1572868
  64.7 0.6 copy-start.5

commit v2 on v1

--- a/solution.py
+++ b/solution.py
@@ -9,31 +9,47 @@
 
 EPS = 1e-06
 MESH = pl.DeviceIdType.MESH
-CHUNKS = 4
+MOST_CHUNKS = 8
 HALF = 128
 
 
 def exchange_kernel(
-    n, m, group_width, scale_rows, blocks,
-    q_ref, k_ref, v_ref, g_ref, sc_ref, taps_ref,
-    conv_out, filt_out, peak_out,
-    zs, zf, ws, wr, tt, gfs, gfr, peak, pks,
-    in_send, in_recv, back_send, back_recv, out_sem, gf_send, gf_recv, pk_send, pk_recv,
+    n, m, chunks, group_width, scale_rows, scale_blocks, blocks,
+    q_in, k_in, v_in, g_in, ex_in, taps_in,
+    prod_out, filt_out, peak_out,
+    q_ref, k_ref, v_ref, g_ref, ex_ref, taps_ref, sc_ref,
+    zs, zf, ws, wr, tt0, tt1, gfs, gfr, peak, pks,
+    load_sem, small_sem,
+    in_send, in_recv, back_send, back_recv, gf_send, gf_recv, pk_send, pk_recv,
 ):
     me = lax.axis_index("ctx")
     row_me = lax.axis_index("ch")
-    channels, rows = q_ref.shape
-    own = channels // n
-    chunk = own // CHUNKS
+    _, own, rows = q_ref.shape
+    chunk = own // chunks
     own_groups = own // group_width
-    chunk_groups = own_groups // CHUNKS
-    scale_blocks = channels // scale_rows
+    chunk_groups = own_groups // chunks
     filter_len = taps_ref.shape[1]
     lead = filter_len // rows
     cols = filter_len // n
     width = filter_len + HALF
     f32 = jnp.float32
 
+    loads = tuple(zip((k_in, v_in, q_in, g_in), (k_ref, v_ref, q_ref, g_ref)))
+
+    def load_copy(i, j):
+        part = pl.ds(pl.multiple_of(j * chunk, 16), chunk)
+        src, dst = loads[i]
+        return pltpu.make_async_copy(src.at[:, part, :], dst.at[:, part, :], load_sem.at[i, j])
+
+    ex_copy = pltpu.make_async_copy(ex_in, ex_ref, small_sem.at[0])
+    taps_copy = pltpu.make_async_copy(taps_in.at[me], taps_ref, small_sem.at[1])
+    ex_copy.start()
+
+    def load_chunk(j, c):
+        for i in range(4):
+            load_copy(i, j).start()
+        return c
+
     barrier = pltpu.get_barrier_semaphore()
 
     def greet_ctx(i, c):
@@ -50,19 +66,32 @@
 
     lax.fori_loop(1, n, greet_ctx, 0)
     lax.fori_loop(1, m, greet_ch, 0)
+    lax.fori_loop(0, chunks, load_chunk, 0)
+    taps_copy.start()
+    ex_copy.wait()
+    per_scale = rows // blocks
+    for a in range(3):
+        scale = jnp.exp2(ex_ref[a].astype(f32))
+        for i in range(scale_blocks):
+            sc_ref[a * scale_blocks + i] = jnp.concatenate(
+                [jnp.broadcast_to(scale[b : b + 1, i : i + 1], (1, per_scale)) for b in range(blocks)], axis=1
+            )
 
     def at_rows(owner, j):
         return pl.ds(pl.multiple_of(owner * own + j * chunk, 16), chunk)
 
+    def at_part(j):
+        return pl.ds(pl.multiple_of(j * chunk, 16), chunk)
+
     def scale_of(which, owner, j):
         return sc_ref[which * scale_blocks + (owner * own + j * chunk) // scale_rows]
 
     def real(ref, which, owner, j):
-        return ref[at_rows(owner, j), :].astype(f32) * scale_of(which, owner, j)
+        return ref[owner, at_part(j), :].astype(f32) * scale_of(which, owner, j)
 
     def mixed(owner, j):
         z = (real(k_ref, 1, owner, j) * real(v_ref, 2, owner, j)).astype(jnp.bfloat16)
-        gw = (real(q_ref, 0, owner, j) * g_ref[at_rows(owner, j), :].astype(f32)).astype(jnp.bfloat16)
+        gw = (real(q_ref, 0, owner, j) * g_ref[owner, at_part(j), :].astype(f32)).astype(jnp.bfloat16)
         return z, gw
 
     def in_copy(j, dst, src):
@@ -105,14 +134,12 @@
             device_id_type=MESH,
         )
 
-    def out_copy(j, owner):
-        return pltpu.make_async_copy(
-            wr.at[:, at_rows(owner, j), :], conv_out.at[:, at_rows(owner, j), :], out_sem.at[j, owner]
-        )
-
     pl.semaphore_wait(barrier, n - 1 + m - 1)
 
     def send_chunk(j, c):
+        for i in range(4):
+            load_copy(i, j).wait()
+
         def one(i, c):
             dst = lax.rem(me + i, n)
             z, gw = mixed(dst, j)
@@ -128,8 +155,9 @@
         zf[me, 1, here, :] = gw
         return c
 
-    lax.fori_loop(0, CHUNKS, send_chunk, 0)
-
+    lax.fori_loop(0, chunks, send_chunk, 0)
+
+    taps_copy.wait()
     peak[...] = jnp.zeros_like(peak)
     flip = (
         lax.broadcasted_iota(jnp.int32, (HALF, HALF), 0)
@@ -142,11 +170,11 @@
         by = (by * group_width) % x.shape[0]
         return x if by == 0 else jnp.concatenate([x[-by:], x[:-by]], axis=0)
 
-    def one_group(gi, c):
+    def one_group(gi, tt):
         at = pl.ds(pl.multiple_of(gi * group_width, 16), group_width)
         z = zf[:, 0, at, :].reshape(n * group_width, rows)
         gw = zf[:, 1, at, :].reshape(n * group_width, rows)
-        taps = taps_ref[pl.ds(me * own_groups + gi, 1), :].astype(jnp.bfloat16).astype(f32)
+        taps = taps_ref[pl.ds(gi, 1), :].astype(jnp.bfloat16).astype(f32)
         line = jnp.concatenate([taps, jnp.zeros((1, HALF), f32)], axis=1)
         band = pltpu.roll(
             jnp.broadcast_to(line, (HALF, width)), 0, 1, stride=1, stride_axis=0
@@ -187,27 +215,25 @@
         lags = jnp.sum(skewed, axis=0, keepdims=True)
         for d in range(n):
             gfs[d, pl.ds(gi, 1), :] = lags[:, d * cols : (d + 1) * cols]
-        return c
 
     def note_peak(j, owner):
         conv = wr[0, at_rows(owner, j), :].astype(f32)
         gz = wr[1, at_rows(owner, j), :].astype(f32)
-        gq = g_ref[at_rows(owner, j), :].astype(f32) * conv
+        gq = g_ref[owner, at_part(j), :].astype(f32) * conv
         gk = gz * real(v_ref, 2, owner, j)
         gv = gz * real(k_ref, 1, owner, j)
         for i, x in enumerate((gq, gk, gv)):
+            prod_out[i, at_rows(owner, j), :] = x
             peak[i] = jnp.maximum(peak[i], jnp.max(jnp.abs(x).reshape(chunk // 8, 8, rows), axis=0))
 
     def take_back(j):
         def one(i, c):
             src = lax.rem(me + n - i, n)
             back_copy(j, me, src).wait_recv()
-            out_copy(j, src).start()
             note_peak(j, src)
             return c
 
         lax.fori_loop(1, n, one, 0)
-        out_copy(j, me).start()
         note_peak(j, me)
 
     def work_chunk(j, c):
@@ -217,7 +243,8 @@
             return c
 
         lax.fori_loop(1, n, arrive, 0)
-        lax.fori_loop(j * chunk_groups, (j + 1) * chunk_groups, one_group, 0)
+        for u in range(chunk_groups):
+            one_group(j * chunk_groups + u, tt1 if u % 2 else tt0)
 
         def reply(i, c):
             back_copy(j, lax.rem(me + i, n), me).start()
@@ -229,7 +256,7 @@
             wr[i, at_rows(me, j), :] = ws[me, i, here, :]
         return c
 
-    lax.fori_loop(0, CHUNKS, work_chunk, 0)
+    lax.fori_loop(0, chunks, work_chunk, 0)
 
     def send_gf(i, c):
         gf_copy(lax.rem(me + i, n), me).start()
@@ -241,7 +268,7 @@
         take_back(j)
         return c
 
-    lax.fori_loop(0, CHUNKS, take_chunk, 0)
+    lax.fori_loop(0, chunks, take_chunk, 0)
 
     for i in range(3):
         lanes = jnp.max(peak[i], axis=0, keepdims=True)
@@ -274,7 +301,7 @@
             back_copy(j, dst, me).wait_send()
             return c
 
-        lax.fori_loop(0, CHUNKS, both, 0)
+        lax.fori_loop(0, chunks, both, 0)
         return c
 
     lax.fori_loop(1, n, settle_ctx, 0)
@@ -288,28 +315,42 @@
     lax.fori_loop(1, m, settle_ch, 0)
     peak_out[...] = jnp.max(pks[...], axis=0)
 
-    def settle_out(j, c):
-        def one(i, c):
-            out_copy(j, i).wait()
-            return c
-
-        lax.fori_loop(0, n, one, 0)
-        return c
-
-    lax.fori_loop(0, CHUNKS, settle_out, 0)
-
-
-def scale_kernel(scale_rows, conv_ref, g_ref, k_ref, v_ref, sc_ref, peak_ref, oq, ok, ov):
-    f32 = jnp.float32
-    inv = 1.0 / (peak_ref[0:3, :] + EPS)
-    conv = conv_ref[0].astype(f32)
-    gz = conv_ref[1].astype(f32)
-    oq[...] = (g_ref[...].astype(f32) * conv * inv[0:1]).astype(jnp.bfloat16)
-    for b in range(g_ref.shape[0] // scale_rows):
-        at = slice(b * scale_rows, (b + 1) * scale_rows)
-        part = gz[at]
-        ok[at, :] = (part * (v_ref[at, :].astype(f32) * sc_ref[1, b]) * inv[1:2]).astype(jnp.bfloat16)
-        ov[at, :] = (part * (k_ref[at, :].astype(f32) * sc_ref[0, b]) * inv[2:3]).astype(jnp.bfloat16)
+
+def scale_kernel(prod, peak, filt, oq, ok, ov, of, op, done, small, sems, small_sems):
+    channels, rows = prod.shape[1:]
+    blocks = small.shape[0]
+    per = rows // blocks
+    outs = (oq, ok, ov)
+    filt_copy = pltpu.make_async_copy(filt, of, small_sems.at[0])
+    filt_copy.start()
+    inv = 1.0 / (peak[0:3, :] + EPS)
+    step = min(256, channels)
+
+    def out_copy(i, r):
+        at = pl.ds(r * step, step)
+        return pltpu.make_async_copy(done.at[i, at, :], outs[i].at[at, :], sems.at[i, r])
+
+    for r in range(channels // step):
+        for i in range(3):
+            at = pl.ds(r * step, step)
+            done[i, at, :] = (prod[i, at, :] * inv[i : i + 1]).astype(jnp.bfloat16)
+            out_copy(i, r).start()
+    at_block = lax.broadcasted_iota(jnp.int32, (blocks, 3), 0)
+    at_kind = lax.broadcasted_iota(jnp.int32, (blocks, 3), 1)
+    table = jnp.zeros((blocks, 3), jnp.float32)
+    for b in range(blocks):
+        for i in range(3):
+            table = jnp.where(
+                (at_block == b) & (at_kind == i), peak[i : i + 1, b * per : b * per + 1], table
+            )
+    small[...] = table
+    peak_copy = pltpu.make_async_copy(small, op, small_sems.at[1])
+    peak_copy.start()
+    for r in range(channels // step):
+        for i in range(3):
+            out_copy(i, r).wait()
+    filt_copy.wait()
+    peak_copy.wait()
 
 
 def shards(n, m, q_vals, k_vals, v_vals, grad_out, exponents, filter_taps):
@@ -320,63 +361,80 @@
     group_width = channels // groups
     own = channels // n
     own_groups = groups // n
+    chunks = min(MOST_CHUNKS, own_groups)
     cols = filter_len // n
     lead = filter_len // rows
     bf16, f32 = jnp.bfloat16, jnp.float32
-    scales = jnp.repeat(jnp.exp2(exponents.astype(f32)), rows // blocks, axis=2)
+    anywhere = pl.BlockSpec(memory_space=pl.ANY)
     vmem = pl.BlockSpec(memory_space=pltpu.VMEM)
     dma = pltpu.SemaphoreType.DMA
-    conv, filt, peak = pl.pallas_call(
-        functools.partial(exchange_kernel, n, m, group_width, scale_rows, blocks),
+    prod, filt, peak = pl.pallas_call(
+        functools.partial(exchange_kernel, n, m, chunks, group_width, scale_rows, scale_blocks, blocks),
         out_shape=(
-            jax.ShapeDtypeStruct((2, channels, rows), bf16),
+            jax.ShapeDtypeStruct((3, channels, rows), f32),
             jax.ShapeDtypeStruct((n, own_groups, cols), f32),
             jax.ShapeDtypeStruct((8, rows), f32),
         ),
-        in_specs=[vmem] * 6,
-        out_specs=(pl.BlockSpec(memory_space=pl.ANY), vmem, vmem),
+        in_specs=[pl.BlockSpec(memory_space=pltpu.HBM)] * 6,
+        out_specs=(vmem, vmem, vmem),
         scratch_shapes=[
+            *[pltpu.VMEM((n, own, rows), bf16) for _ in range(4)],
+            pltpu.VMEM((3, blocks, scale_blocks), jnp.int32),
+            pltpu.VMEM((own_groups, filter_len), f32),
+            pltpu.VMEM((3 * scale_blocks, 1, rows), f32),
             pltpu.VMEM((2, channels, rows), bf16),
             pltpu.VMEM((n, 2, own, rows), bf16),
             pltpu.VMEM((n, 2, own, rows), bf16),
             pltpu.VMEM((2, channels, rows), bf16),
             pltpu.VMEM(((lead + 1) * rows, rows), bf16),
+            pltpu.VMEM(((lead + 1) * rows, rows), bf16),
             pltpu.VMEM((n, own_groups, cols), f32),
             pltpu.VMEM((n, own_groups, cols), f32),
             pltpu.VMEM((3, 8, rows), f32),
             pltpu.VMEM((m, 8, rows), f32),
-            dma((CHUNKS, n)),
-            dma((CHUNKS, n)),
-            dma((CHUNKS, n)),
-            dma((CHUNKS, n)),
-            dma((CHUNKS, n)),
+            dma((4, chunks)),
+            dma((2,)),
+            dma((chunks, n)),
+            dma((chunks, n)),
+            dma((chunks, n)),
+            dma((chunks, n)),
             dma((n,)),
             dma((n,)),
             dma((m,)),
             dma((m,)),
         ],
         compiler_params=pltpu.CompilerParams(
-            collective_id=0, has_side_effects=True, vmem_limit_bytes=48 * 1024 * 1024
+            collective_id=0, has_side_effects=True, vmem_limit_bytes=32 * 1024 * 1024
         ),
     )(
-        q_vals, k_vals, v_vals, grad_out,
-        scales.reshape(3 * scale_blocks, 1, rows), filter_taps,
+        *[
+            pltpu.with_memory_space_constraint(x, pltpu.HBM)
+            for x in (
+                *[x.reshape(n, own, rows) for x in (q_vals, k_vals, v_vals, grad_out)],
+                exponents.transpose(0, 2, 1),
+                filter_taps.reshape(n, own_groups, filter_len),
+            )
+        ]
     )
-    tile = min(256, channels)
-    flat = pl.BlockSpec((tile, rows), lambda i: (i, 0))
-    grads = pl.pallas_call(
-        functools.partial(scale_kernel, scale_rows),
-        grid=(channels // tile,),
-        out_shape=tuple(jax.ShapeDtypeStruct((channels, rows), bf16) for _ in range(3)),
-        in_specs=[
-            pl.BlockSpec((2, tile, rows), lambda i: (0, i, 0)),
+    flat = jax.ShapeDtypeStruct((channels, rows), bf16)
+    *grads, filt, peak = pl.pallas_call(
+        scale_kernel,
+        out_shape=(
             flat, flat, flat,
-            pl.BlockSpec((2, tile // scale_rows, 1, rows), lambda i: (0, i, 0, 0)),
-            pl.BlockSpec((8, rows), lambda i: (0, 0)),
+            jax.ShapeDtypeStruct((n, own_groups, cols), f32),
+            jax.ShapeDtypeStruct((blocks, 3), f32),
+        ),
+        in_specs=[vmem] * 3,
+        out_specs=[anywhere] * 5,
+        scratch_shapes=[
+            pltpu.VMEM((3, channels, rows), bf16),
+            pltpu.VMEM((blocks, 3), f32),
+            dma((3, channels // min(256, channels))),
+            dma((2,)),
         ],
-        out_specs=(flat, flat, flat),
-    )(conv, grad_out, k_vals, v_vals, scales[1:3].reshape(2, scale_blocks, 1, rows), peak)
-    return (*grads, filt.reshape(groups, cols), peak[0:3, :: rows // blocks])
+        compiler_params=pltpu.CompilerParams(vmem_limit_bytes=16 * 1024 * 1024),
+    )(prod, peak, filt)
+    return (*grads, filt.reshape(groups, cols), peak.T)
 
 
 def solution(mesh):

time: 75.3 us -> 61.4 us (0.82)
  local copies, waits for them, and re-layouts: 9.6 us -> 0 us
  Pallas kernels: 63.8 us -> 60.6 us
    unnamed x14 -> x0, local copies, waits for them, and re-layouts: 7.8 us -> none
    pallas_call x2, Pallas kernels: 63.8 us -> 60.6 us  [the longest x1 58.7 us: shards(): pl.pallas_call(functools.partial(exchange_kernel, n, m, chunks, group_wid...]
    slice x3 -> x0, local copies, waits for them, and re-layouts: 0.87 us -> none  [the longest x1 0.78 us: shards(): return (*grads, filt.reshape(groups, cols), peak[0:3, ::rows // blocks])]
    broadcast_in_dim x2 -> x0, local copies, waits for them, and re-layouts: 0.83 us -> none  [shards(): scales = jnp.repeat(jnp.exp2(exponents.astype(f32)), rows // blocks, axis=2)]
where the time goes in v2:
time: 61.4 us; the launch traced here: 61.3 us
  Pallas kernels  60.6 us (99%)
  between operations  0.64 us (1%)
    pallas_call x1, Pallas kernels, shards(): pl.pallas_call(functools.partial(exchange_kernel, n, m, chunks, group_wid...  58.7 us
    pallas_call x1, Pallas kernels, shards(): pl.pallas_call(scale_kernel, out_shape=(flat, flat, flat, jax.ShapeDtypeS...  1.9 us

profile of v2, /device:TPU:0, one launch (start us, length us, event | category | flops | bytes accessed | tf_op | source)
XLA Modules:
  0.0 61.3 jit_solution(10223118444940423123)
XLA Ops:
  0.6 58.7 %shard_map.101 = (f32[3,2048,256]{2,1,0:T(8,128)S(1)}, f32[8,16,128]{2,1,0:T(8,128)S(1)}, f32[8,256]{1,0:T(8,128)S(1)}) custom-call(bf16[8,256,256]{2,1,0:T(8,128)(2,1)} %bitcast.8, bf16[8,256,256]{2,1,0:T(8,128)(2,1)} %bitcast.9, bf16[8,256,256]{2,1,0:T(8,128)(2,1)} %bitcast.10, bf16[8,256,256]{2,1,0:T(8,128)(2,1)} %bitcast.11, s32[3,2,16]{2,1,0:T(2,128)} %bitcast.13, ...), custom_call_target="tpu_custom_call" | custom-call | tf_op jit(solution)/shard_map/pallas_call | solution.py:371
  59.4 1.9 %shard_map.102 = (bf16[2048,256]{1,0:T(8,128)(2,1)}, bf16[2048,256]{1,0:T(8,128)(2,1)}, bf16[2048,256]{1,0:T(8,128)(2,1)}, f32[8,16,128]{2,1,0:T(8,128)}, f32[2,3]{1,0:T(2,128)}) custom-call(f32[3,2048,256]{2,1,0:T(8,128)S(1)} %get-tuple-element.13.prod, f32[8,256]{1,0:T(8,128)S(1)} %get-tuple-element.14.peak, f32[8,16,128]{2,1,0:T(8,128)S(1)} %get-tuple-element.15.filt), custom_call_target="tpu_custom_call" | custom-call | tf_op jit(solution)/shard_map/pallas_call | solution.py:420

commit v3 on v2

--- a/solution.py
+++ b/solution.py
@@ -33,6 +33,22 @@
     cols = filter_len // n
     width = filter_len + HALF
     f32 = jnp.float32
+    chips = n // 2
+
+    def flipped(mask):
+        out, bit = 0, 1
+        while bit < n:
+            out = out + lax.rem(lax.div(me, bit) + lax.div(mask, bit), 2) * bit
+            bit *= 2
+        return out
+
+    core = lax.rem(me, 2)
+    peers = []
+    for low in range(2):
+        for h in range(1, chips):
+            swap = (1 if h == 1 else -1 if h == 2 else 0) if chips > 2 else 0
+            peers.append(flipped((h + core * swap) * 2 + low))
+    peers.append(flipped(jnp.int32(1)))
 
     loads = tuple(zip((k_in, v_in, q_in, g_in), (k_ref, v_ref, q_ref, g_ref)))
 
@@ -140,15 +156,11 @@
         for i in range(4):
             load_copy(i, j).wait()
 
-        def one(i, c):
-            dst = lax.rem(me + i, n)
+        for dst in peers:
             z, gw = mixed(dst, j)
             zs[0, at_rows(dst, j), :] = z
             zs[1, at_rows(dst, j), :] = gw
             in_copy(j, dst, me).start()
-            return c
-
-        lax.fori_loop(1, n, one, 0)
         z, gw = mixed(me, j)
         here = pl.ds(pl.multiple_of(j * chunk, 16), chunk)
         zf[me, 0, here, :] = z
@@ -227,30 +239,19 @@
             peak[i] = jnp.maximum(peak[i], jnp.max(jnp.abs(x).reshape(chunk // 8, 8, rows), axis=0))
 
     def take_back(j):
-        def one(i, c):
-            src = lax.rem(me + n - i, n)
+        for src in peers:
             back_copy(j, me, src).wait_recv()
             note_peak(j, src)
-            return c
-
-        lax.fori_loop(1, n, one, 0)
         note_peak(j, me)
 
     def work_chunk(j, c):
-        def arrive(i, c):
-            src = lax.rem(me + n - i, n)
+        for src in peers:
             in_copy(j, me, src).wait_recv()
-            return c
-
-        lax.fori_loop(1, n, arrive, 0)
         for u in range(chunk_groups):
             one_group(j * chunk_groups + u, tt1 if u % 2 else tt0)
 
-        def reply(i, c):
-            back_copy(j, lax.rem(me + i, n), me).start()
-            return c
-
-        lax.fori_loop(1, n, reply, 0)
+        for dst in peers:
+            back_copy(j, dst, me).start()
         here = pl.ds(pl.multiple_of(j * chunk, 16), chunk)
         for i in range(2):
             wr[i, at_rows(me, j), :] = ws[me, i, here, :]

time: 61.4 us -> 61.5 us (level)
  no operation moved by 1% of the time
where the time goes in v3:
time: 61.5 us; the launch traced here: 61.3 us
  Pallas kernels  60.6 us (99%)
  between operations  0.64 us (1%)
    pallas_call x1, Pallas kernels, shards(): pl.pallas_call(functools.partial(exchange_kernel, n, m, chunks, group_wid...  58.7 us
    pallas_call x1, Pallas kernels, shards(): pl.pallas_call(scale_kernel, out_shape=(flat, flat, flat, jax.ShapeDtypeS...  1.9 us

profile of v3, /device:TPU:0, one launch (start us, length us, event | category | flops | bytes accessed | tf_op | source)
XLA Modules:
  0.0 61.3 jit_solution(7301802244939395540)
XLA Ops:
  0.6 58.7 %shard_map.101 = (f32[3,2048,256]{2,1,0:T(8,128)S(1)}, f32[8,16,128]{2,1,0:T(8,128)S(1)}, f32[8,256]{1,0:T(8,128)S(1)}) custom-call(bf16[8,256,256]{2,1,0:T(8,128)(2,1)} %bitcast.8, bf16[8,256,256]{2,1,0:T(8,128)(2,1)} %bitcast.9, bf16[8,256,256]{2,1,0:T(8,128)(2,1)} %bitcast.10, bf16[8,256,256]{2,1,0:T(8,128)(2,1)} %bitcast.11, s32[3,2,16]{2,1,0:T(2,128)} %bitcast.13, ...), custom_call_target="tpu_custom_call" | custom-call | tf_op jit(solution)/shard_map/pallas_call | solution.py:372
  59.4 1.9 %shard_map.102 = (bf16[2048,256]{1,0:T(8,128)(2,1)}, bf16[2048,256]{1,0:T(8,128)(2,1)}, bf16[2048,256]{1,0:T(8,128)(2,1)}, f32[8,16,128]{2,1,0:T(8,128)}, f32[2,3]{1,0:T(2,128)}) custom-call(f32[3,2048,256]{2,1,0:T(8,128)S(1)} %get-tuple-element.13.prod, f32[8,256]{1,0:T(8,128)S(1)} %get-tuple-element.14.peak, f32[8,16,128]{2,1,0:T(8,128)S(1)} %get-tuple-element.15.filt), custom_call_target="tpu_custom_call" | custom-call | tf_op jit(solution)/shard_map/pallas_call | solution.py:421

commit v4 on v3

--- a/solution.py
+++ b/solution.py
@@ -18,7 +18,7 @@
     q_in, k_in, v_in, g_in, ex_in, taps_in,
     prod_out, filt_out, peak_out,
     q_ref, k_ref, v_ref, g_ref, ex_ref, taps_ref, sc_ref,
-    zs, zf, ws, wr, tt0, tt1, gfs, gfr, peak, pks,
+    zs, zf, ws, wr, tt0, tt1, flip_ref, lags, gfs, gfr, peak, pks,
     load_sem, small_sem,
     in_send, in_recv, back_send, back_recv, gf_send, gf_recv, pk_send, pk_recv,
 ):
@@ -171,11 +171,12 @@
 
     taps_copy.wait()
     peak[...] = jnp.zeros_like(peak)
-    flip = (
-        lax.broadcasted_iota(jnp.int32, (HALF, HALF), 0)
-        + lax.broadcasted_iota(jnp.int32, (HALF, HALF), 1)
-        == HALF - 1
-    ).astype(f32).astype(jnp.bfloat16)
+    def mirror(size, kind):
+        at = lax.broadcasted_iota(jnp.int32, (size, size), 0)
+        to = lax.broadcasted_iota(jnp.int32, (size, size), 1)
+        return (at + to == size - 1).astype(f32).astype(kind)
+
+    flip_ref[...] = mirror(rows, jnp.bfloat16)
     zero = jnp.zeros((HALF, HALF), jnp.bfloat16)
 
     def turned(x, by):
@@ -204,29 +205,29 @@
                     tt[o * rows + a * HALF : o * rows + (a + 1) * HALF, b * HALF : (b + 1) * HALF] = tile(
                         o * per + b - a
                     )
-        zwin = jnp.concatenate([turned(z, o) for o in range(lead + 1)], axis=1)
-        w = jnp.dot(zwin, tt[...], preferred_element_type=f32)
+        gw = jnp.dot(gw, flip_ref[...], preferred_element_type=f32).astype(jnp.bfloat16)
         gparts = [turned(gw, -o) for o in range(lead + 1)]
-        gz = jnp.zeros((n * group_width, rows), f32)
-        for o in range(lead + 1):
-            gz = gz + lax.dot_general(
-                gparts[o], tt[o * rows : (o + 1) * rows, :], (((1,), (1,)), ((), ())),
-                preferred_element_type=f32,
-            )
-        ws[:, 0, at, :] = w.astype(jnp.bfloat16).reshape(n, group_width, rows)
+        both = jnp.concatenate(
+            [
+                jnp.concatenate([turned(z, o) for o in range(lead + 1)], axis=1),
+                jnp.concatenate(gparts, axis=1),
+            ],
+            axis=0,
+        )
+        res = jnp.dot(both, tt[...], preferred_element_type=f32).astype(jnp.bfloat16)
+        w = res[: n * group_width]
+        gz = jnp.dot(res[n * group_width :], flip_ref[...], preferred_element_type=f32)
+        ws[:, 0, at, :] = w.reshape(n, group_width, rows)
         ws[:, 1, at, :] = gz.astype(jnp.bfloat16).reshape(n, group_width, rows)
 
-        gwin = jnp.concatenate(gparts, axis=1)
+        gwin = jnp.concatenate(gparts[::-1], axis=1)
         zcat = jnp.concatenate([z[:, a * HALF : (a + 1) * HALF] for a in range(per)], axis=0)
-        gcat = jnp.concatenate([gwin[:, a * HALF : a * HALF + width] for a in range(per)], axis=0)
-        zrev = lax.dot_general(
-            flip, zcat, (((1,), (1,)), ((), ())), preferred_element_type=f32
-        ).astype(jnp.bfloat16)
-        cross = jnp.dot(zrev, gcat, preferred_element_type=f32)
-        skewed = pltpu.roll(cross, width - (HALF - 1), 1, stride=1, stride_axis=0)
-        lags = jnp.sum(skewed, axis=0, keepdims=True)
-        for d in range(n):
-            gfs[d, pl.ds(gi, 1), :] = lags[:, d * cols : (d + 1) * cols]
+        gcat = jnp.concatenate(
+            [gwin[:, (per - 1 - a) * HALF : (per - 1 - a) * HALF + width] for a in range(per)], axis=0
+        )
+        cross = lax.dot_general(zcat, gcat, (((0,), (0,)), ((), ())), preferred_element_type=f32)
+        skewed = pltpu.roll(cross, 0, 1, stride=1, stride_axis=0)
+        lags[pl.ds(gi, 1), :] = jnp.sum(skewed, axis=0, keepdims=True)[:, HALF:]
 
     def note_peak(j, owner):
         conv = wr[0, at_rows(owner, j), :].astype(f32)
@@ -258,6 +259,19 @@
         return c
 
     lax.fori_loop(0, chunks, work_chunk, 0)
+
+    back = mirror(HALF, f32)
+    straight = jnp.concatenate(
+        [
+            jnp.dot(
+                lags[:, i : i + HALF], back, preferred_element_type=f32, precision=lax.Precision.HIGHEST
+            )
+            for i in range(filter_len - HALF, -1, -HALF)
+        ],
+        axis=1,
+    )
+    for d in range(n):
+        gfs[d] = straight[:, d * cols : (d + 1) * cols]
 
     def send_gf(i, c):
         gf_copy(lax.rem(me + i, n), me).start()
@@ -389,6 +403,8 @@
             pltpu.VMEM((2, channels, rows), bf16),
             pltpu.VMEM(((lead + 1) * rows, rows), bf16),
             pltpu.VMEM(((lead + 1) * rows, rows), bf16),
+            pltpu.VMEM((rows, rows), bf16),
+            pltpu.VMEM((own_groups, filter_len), f32),
             pltpu.VMEM((n, own_groups, cols), f32),
             pltpu.VMEM((n, own_groups, cols), f32),
             pltpu.VMEM((3, 8, rows), f32),

time: 61.5 us -> 61.5 us (level)
  no operation moved by 1% of the time
where the time goes in v4:
time: 61.5 us; the launch traced here: 61.3 us
  Pallas kernels  60.6 us (99%)
  between operations  0.64 us (1%)
    pallas_call x1, Pallas kernels, shards(): pl.pallas_call(functools.partial(exchange_kernel, n, m, chunks, group_wid...  58.7 us
    pallas_call x1, Pallas kernels, shards(): pl.pallas_call(scale_kernel, out_shape=(flat, flat, flat, jax.ShapeDtypeS...  1.9 us

profile of v4, /device:TPU:0, one launch (start us, length us, event | category | flops | bytes accessed | tf_op | source)
XLA Modules:
  0.0 61.3 jit_solution(11264575978431269183)
XLA Ops:
  0.6 58.7 %shard_map.101 = (f32[3,2048,256]{2,1,0:T(8,128)S(1)}, f32[8,16,128]{2,1,0:T(8,128)S(1)}, f32[8,256]{1,0:T(8,128)S(1)}) custom-call(bf16[8,256,256]{2,1,0:T(8,128)(2,1)} %bitcast.8, bf16[8,256,256]{2,1,0:T(8,128)(2,1)} %bitcast.9, bf16[8,256,256]{2,1,0:T(8,128)(2,1)} %bitcast.10, bf16[8,256,256]{2,1,0:T(8,128)(2,1)} %bitcast.11, s32[3,2,16]{2,1,0:T(2,128)} %bitcast.13, ...), custom_call_target="tpu_custom_call" | custom-call | tf_op jit(solution)/shard_map/pallas_call | solution.py:386
  59.4 1.9 %shard_map.102 = (bf16[2048,256]{1,0:T(8,128)(2,1)}, bf16[2048,256]{1,0:T(8,128)(2,1)}, bf16[2048,256]{1,0:T(8,128)(2,1)}, f32[8,16,128]{2,1,0:T(8,128)}, f32[2,3]{1,0:T(2,128)}) custom-call(f32[3,2048,256]{2,1,0:T(8,128)S(1)} %get-tuple-element.13.prod, f32[8,256]{1,0:T(8,128)S(1)} %get-tuple-element.14.peak, f32[8,16,128]{2,1,0:T(8,128)S(1)} %get-tuple-element.15.filt), custom_call_target="tpu_custom_call" | custom-call | tf_op jit(solution)/shard_map/pallas_call | solution.py:437

commit v5 on v4

--- a/solution.py
+++ b/solution.py
@@ -10,6 +10,7 @@
 EPS = 1e-06
 MESH = pl.DeviceIdType.MESH
 MOST_CHUNKS = 8
+AHEAD = 4
 HALF = 128
 
 
@@ -82,8 +83,7 @@
 
     lax.fori_loop(1, n, greet_ctx, 0)
     lax.fori_loop(1, m, greet_ch, 0)
-    lax.fori_loop(0, chunks, load_chunk, 0)
-    taps_copy.start()
+    load_chunk(0, 0)
     ex_copy.wait()
     per_scale = rows // blocks
     for a in range(3):
@@ -150,12 +150,13 @@
             device_id_type=MESH,
         )
 
+    for i in range(4):
+        load_copy(i, 0).wait()
+    lax.fori_loop(1, chunks, load_chunk, 0)
+    taps_copy.start()
     pl.semaphore_wait(barrier, n - 1 + m - 1)
 
     def send_chunk(j, c):
-        for i in range(4):
-            load_copy(i, j).wait()
-
         for dst in peers:
             z, gw = mixed(dst, j)
             zs[0, at_rows(dst, j), :] = z
@@ -167,7 +168,14 @@
         zf[me, 1, here, :] = gw
         return c
 
-    lax.fori_loop(0, chunks, send_chunk, 0)
+    def load_and_send(j, c):
+        for i in range(4):
+            load_copy(i, j).wait()
+        return send_chunk(j, c)
+
+    ahead = min(AHEAD, chunks)
+    send_chunk(0, 0)
+    lax.fori_loop(1, ahead, load_and_send, 0)
 
     taps_copy.wait()
     peak[...] = jnp.zeros_like(peak)
@@ -248,6 +256,7 @@
     def work_chunk(j, c):
         for src in peers:
             in_copy(j, me, src).wait_recv()
+        pl.when(j + ahead < chunks)(lambda: load_and_send(j + ahead, None))
         for u in range(chunk_groups):
             one_group(j * chunk_groups + u, tt1 if u % 2 else tt0)
 

time: 61.5 us -> 61.5 us (level)
  no operation moved by 1% of the time
where the time goes in v5:
time: 61.5 us; the launch traced here: 61.3 us
  Pallas kernels  60.7 us (99%)
  between operations  0.64 us (1%)
    pallas_call x1, Pallas kernels, shards(): pl.pallas_call(functools.partial(exchange_kernel, n, m, chunks, group_wid...  58.8 us
    pallas_call x1, Pallas kernels, shards(): pl.pallas_call(scale_kernel, out_shape=(flat, flat, flat, jax.ShapeDtypeS...  1.9 us

profile of v5, /device:TPU:0, one launch (start us, length us, event | category | flops | bytes accessed | tf_op | source)
XLA Modules:
  0.0 61.3 jit_solution(564335732805683972)
XLA Ops:
  0.6 58.8 %shard_map.101 = (f32[3,2048,256]{2,1,0:T(8,128)S(1)}, f32[8,16,128]{2,1,0:T(8,128)S(1)}, f32[8,256]{1,0:T(8,128)S(1)}) custom-call(bf16[8,256,256]{2,1,0:T(8,128)(2,1)} %bitcast.8, bf16[8,256,256]{2,1,0:T(8,128)(2,1)} %bitcast.9, bf16[8,256,256]{2,1,0:T(8,128)(2,1)} %bitcast.10, bf16[8,256,256]{2,1,0:T(8,128)(2,1)} %bitcast.11, s32[3,2,16]{2,1,0:T(2,128)} %bitcast.13, ...), custom_call_target="tpu_custom_call" | custom-call | tf_op jit(solution)/shard_map/pallas_call | solution.py:395
  59.4 1.9 %shard_map.102 = (bf16[2048,256]{1,0:T(8,128)(2,1)}, bf16[2048,256]{1,0:T(8,128)(2,1)}, bf16[2048,256]{1,0:T(8,128)(2,1)}, f32[8,16,128]{2,1,0:T(8,128)}, f32[2,3]{1,0:T(2,128)}) custom-call(f32[3,2048,256]{2,1,0:T(8,128)S(1)} %get-tuple-element.13.prod, f32[8,256]{1,0:T(8,128)S(1)} %get-tuple-element.14.peak, f32[8,16,128]{2,1,0:T(8,128)S(1)} %get-tuple-element.15.filt), custom_call_target="tpu_custom_call" | custom-call | tf_op jit(solution)/shard_map/pallas_call | solution.py:446

commit v6 on v5

--- a/solution.py
+++ b/solution.py
@@ -20,7 +20,7 @@
     prod_out, filt_out, peak_out,
     q_ref, k_ref, v_ref, g_ref, ex_ref, taps_ref, sc_ref,
     zs, zf, ws, wr, tt0, tt1, flip_ref, lags, gfs, gfr, peak, pks,
-    load_sem, small_sem,
+    rel_in, rel_back, rel_sem, load_sem, small_sem,
     in_send, in_recv, back_send, back_recv, gf_send, gf_recv, pk_send, pk_recv,
 ):
     me = lax.axis_index("ctx")
@@ -44,12 +44,21 @@
         return out
 
     core = lax.rem(me, 2)
+    relayed = chips == 4
     peers = []
     for low in range(2):
         for h in range(1, chips):
             swap = (1 if h == 1 else -1 if h == 2 else 0) if chips > 2 else 0
-            peers.append(flipped((h + core * swap) * 2 + low))
+            if not (relayed and h == 3):
+                peers.append(flipped((h + core * swap) * 2 + low))
     peers.append(flipped(jnp.int32(1)))
+    direct = list(peers)
+    far, onward = [], []
+    if relayed:
+        via = flipped((1 + core) * 2)
+        far = [flipped(jnp.int32(6 + low)) for low in range(2)]
+        onward = [flipped((2 - core) * 2 + low) for low in range(2)]
+        peers = peers + far
 
     loads = tuple(zip((k_in, v_in, q_in, g_in), (k_ref, v_ref, q_ref, g_ref)))
 
@@ -130,6 +139,56 @@
             device_id_type=MESH,
         )
 
+    def in_relay(j, low):
+        return pltpu.make_async_remote_copy(
+            src_ref=zs.at[:, at_rows(far[low], j), :],
+            dst_ref=rel_in.at[j, low],
+            send_sem=in_send.at[j, far[low]],
+            recv_sem=rel_sem.at[0, j, low],
+            device_id={"ctx": via},
+            device_id_type=MESH,
+        )
+
+    def in_onward(j, low):
+        return pltpu.make_async_remote_copy(
+            src_ref=rel_in.at[j, low],
+            dst_ref=zf.at[via, :, at_part(j), :],
+            send_sem=rel_sem.at[1, j, low],
+            recv_sem=in_recv.at[j, via],
+            device_id={"ctx": onward[low]},
+            device_id_type=MESH,
+        )
+
+    def back_relay(j, low):
+        return pltpu.make_async_remote_copy(
+            src_ref=ws.at[far[low], :, at_part(j), :],
+            dst_ref=rel_back.at[j, low],
+            send_sem=back_send.at[j, far[low]],
+            recv_sem=rel_sem.at[2, j, low],
+            device_id={"ctx": via},
+            device_id_type=MESH,
+        )
+
+    def back_onward(j, low):
+        return pltpu.make_async_remote_copy(
+            src_ref=rel_back.at[j, low],
+            dst_ref=wr.at[:, at_rows(via, j), :],
+            send_sem=rel_sem.at[3, j, low],
+            recv_sem=back_recv.at[j, via],
+            device_id={"ctx": onward[low]},
+            device_id_type=MESH,
+        )
+
+    def pass_in(j):
+        for low in range(len(far)):
+            in_relay(j, low).wait_recv()
+            in_onward(j, low).start()
+
+    def pass_back(j):
+        for low in range(len(far)):
+            back_relay(j, low).wait_recv()
+            back_onward(j, low).start()
+
     def gf_copy(dst, src):
         return pltpu.make_async_remote_copy(
             src_ref=gfs.at[dst],
@@ -157,11 +216,11 @@
     pl.semaphore_wait(barrier, n - 1 + m - 1)
 
     def send_chunk(j, c):
-        for dst in peers:
+        for low, dst in [*enumerate(far), *((None, d) for d in direct)]:
             z, gw = mixed(dst, j)
             zs[0, at_rows(dst, j), :] = z
             zs[1, at_rows(dst, j), :] = gw
-            in_copy(j, dst, me).start()
+            (in_copy(j, dst, me) if low is None else in_relay(j, low)).start()
         z, gw = mixed(me, j)
         here = pl.ds(pl.multiple_of(j * chunk, 16), chunk)
         zf[me, 0, here, :] = z
@@ -259,15 +318,22 @@
         pl.when(j + ahead < chunks)(lambda: load_and_send(j + ahead, None))
         for u in range(chunk_groups):
             one_group(j * chunk_groups + u, tt1 if u % 2 else tt0)
-
-        for dst in peers:
+            if u == 0:
+                pl.when(j + 1 < chunks)(lambda: pass_in(j + 1))
+                pl.when(j > 0)(lambda: pass_back(j - 1))
+
+        for low in range(len(far)):
+            back_relay(j, low).start()
+        for dst in direct:
             back_copy(j, dst, me).start()
         here = pl.ds(pl.multiple_of(j * chunk, 16), chunk)
         for i in range(2):
             wr[i, at_rows(me, j), :] = ws[me, i, here, :]
         return c
 
+    pass_in(0)
     lax.fori_loop(0, chunks, work_chunk, 0)
+    pass_back(chunks - 1)
 
     back = mirror(HALF, f32)
     straight = jnp.concatenate(
@@ -313,6 +379,14 @@
     lax.fori_loop(1, m, send_pk, 0)
 
     gfr[me] = gfs[me]
+
+    def settle_relay(j, c):
+        for low in range(len(far)):
+            in_onward(j, low).wait_send()
+            back_onward(j, low).wait_send()
+        return c
+
+    lax.fori_loop(0, chunks, settle_relay, 0)
 
     def settle_ctx(i, c):
         dst = lax.rem(me + i, n)
@@ -418,6 +492,9 @@
             pltpu.VMEM((n, own_groups, cols), f32),
             pltpu.VMEM((3, 8, rows), f32),
             pltpu.VMEM((m, 8, rows), f32),
+            pltpu.VMEM((chunks, 2, 2, own // chunks, rows), bf16),
+            pltpu.VMEM((chunks, 2, 2, own // chunks, rows), bf16),
+            dma((4, chunks, 2)),
             dma((4, chunks)),
             dma((2,)),
             dma((chunks, n)),

time: 61.5 us -> 67 us (1.089)
  Pallas kernels: 60.7 us -> 66.2 us
    pallas_call x1, Pallas kernels: 58.8 us -> 64.3 us  [shards(): pl.pallas_call(functools.partial(exchange_kernel, n, m, chunks, group_wid...]
where the time goes in v6:
time: 67 us; the launch traced here: 66.8 us
  Pallas kernels  66.2 us (99%)
    pallas_call x1, Pallas kernels, shards(): pl.pallas_call(functools.partial(exchange_kernel, n, m, chunks, group_wid...  64.3 us
    pallas_call x1, Pallas kernels, shards(): pl.pallas_call(scale_kernel, out_shape=(flat, flat, flat, jax.ShapeDtypeS...  1.9 us

profile of v6, /device:TPU:0, one launch (start us, length us, event | category | flops | bytes accessed | tf_op | source)
XLA Modules:
  0.0 66.8 jit_solution(15269485256376625684)
XLA Ops:
  0.6 64.3 %shard_map.101 = (f32[3,2048,256]{2,1,0:T(8,128)S(1)}, f32[8,16,128]{2,1,0:T(8,128)S(1)}, f32[8,256]{1,0:T(8,128)S(1)}) custom-call(bf16[8,256,256]{2,1,0:T(8,128)(2,1)} %bitcast.8, bf16[8,256,256]{2,1,0:T(8,128)(2,1)} %bitcast.9, bf16[8,256,256]{2,1,0:T(8,128)(2,1)} %bitcast.10, bf16[8,256,256]{2,1,0:T(8,128)(2,1)} %bitcast.11, s32[3,2,16]{2,1,0:T(2,128)} %bitcast.13, ...), custom_call_target="tpu_custom_call" | custom-call | tf_op jit(solution)/shard_map/pallas_call | solution.py:469
  64.9 1.9 %shard_map.102 = (bf16[2048,256]{1,0:T(8,128)(2,1)}, bf16[2048,256]{1,0:T(8,128)(2,1)}, bf16[2048,256]{1,0:T(8,128)(2,1)}, f32[8,16,128]{2,1,0:T(8,128)}, f32[2,3]{1,0:T(2,128)}) custom-call(f32[3,2048,256]{2,1,0:T(8,128)S(1)} %get-tuple-element.13.prod, f32[8,256]{1,0:T(8,128)S(1)} %get-tuple-element.14.peak, f32[8,16,128]{2,1,0:T(8,128)S(1)} %get-tuple-element.15.filt), custom_call_target="tpu_custom_call" | custom-call | tf_op jit(solution)/shard_map/pallas_call | solution.py:523

commit v7 on v4

--- a/solution.py
+++ b/solution.py
@@ -43,12 +43,25 @@
         return out
 
     core = lax.rem(me, 2)
-    peers = []
-    for low in range(2):
-        for h in range(1, chips):
-            swap = (1 if h == 1 else -1 if h == 2 else 0) if chips > 2 else 0
-            peers.append(flipped((h + core * swap) * 2 + low))
-    peers.append(flipped(jnp.int32(1)))
+    one_hop = [flipped(jnp.int32(x)) for x in ((4, 5) if chips == 4 else ())]
+    others = [flipped(jnp.int32(x)) for x in ((2, 6, 3, 7) if chips == 4 else range(2, n))]
+    mate = flipped(jnp.int32(1))
+    peers = one_hop + others + [mate]
+
+    def by_core(even, odd, act):
+        for parity, dsts in ((0, even), (1, odd)):
+
+            @pl.when(core == parity)
+            def _(dsts=dsts):
+                for dst in dsts:
+                    act(dst)
+
+    def over_chunks(act):
+        def one(j, c):
+            act(j)
+            return c
+
+        lax.fori_loop(0, chunks, one, 0)
 
     loads = tuple(zip((k_in, v_in, q_in, g_in), (k_ref, v_ref, q_ref, g_ref)))
 
@@ -160,7 +173,8 @@
             z, gw = mixed(dst, j)
             zs[0, at_rows(dst, j), :] = z
             zs[1, at_rows(dst, j), :] = gw
-            in_copy(j, dst, me).start()
+        by_core(one_hop, others, lambda dst: in_copy(j, dst, me).start())
+        in_copy(j, mate, me).start()
         z, gw = mixed(me, j)
         here = pl.ds(pl.multiple_of(j * chunk, 16), chunk)
         zf[me, 0, here, :] = z
@@ -168,6 +182,8 @@
         return c
 
     lax.fori_loop(0, chunks, send_chunk, 0)
+    over_chunks(lambda j: by_core(one_hop, others, lambda dst: in_copy(j, dst, me).wait_send()))
+    over_chunks(lambda j: by_core(others, one_hop, lambda dst: in_copy(j, dst, me).start()))
 
     taps_copy.wait()
     peak[...] = jnp.zeros_like(peak)
@@ -251,14 +267,16 @@
         for u in range(chunk_groups):
             one_group(j * chunk_groups + u, tt1 if u % 2 else tt0)
 
-        for dst in peers:
-            back_copy(j, dst, me).start()
+        by_core(others, one_hop, lambda dst: back_copy(j, dst, me).start())
+        back_copy(j, mate, me).start()
         here = pl.ds(pl.multiple_of(j * chunk, 16), chunk)
         for i in range(2):
             wr[i, at_rows(me, j), :] = ws[me, i, here, :]
         return c
 
     lax.fori_loop(0, chunks, work_chunk, 0)
+    over_chunks(lambda j: by_core(others, one_hop, lambda dst: back_copy(j, dst, me).wait_send()))
+    over_chunks(lambda j: by_core(one_hop, others, lambda dst: back_copy(j, dst, me).start()))
 
     back = mirror(HALF, f32)
     straight = jnp.concatenate(
@@ -311,15 +329,17 @@
         gf_copy(me, src).wait_recv()
         gf_copy(dst, me).wait_send()
 
-        def both(j, c):
-            in_copy(j, dst, me).wait_send()
-            back_copy(j, dst, me).wait_send()
-            return c
-
-        lax.fori_loop(0, chunks, both, 0)
         return c
 
     lax.fori_loop(1, n, settle_ctx, 0)
+    over_chunks(lambda j: by_core(others, one_hop, lambda dst: in_copy(j, dst, me).wait_send()))
+    over_chunks(lambda j: by_core(one_hop, others, lambda dst: back_copy(j, dst, me).wait_send()))
+
+    def settle_mate(j):
+        in_copy(j, mate, me).wait_send()
+        back_copy(j, mate, me).wait_send()
+
+    over_chunks(settle_mate)
     filt_out[...] = gfr[...]
 
     def settle_ch(i, c):

time: 61.5 us -> 65.7 us (1.068)
  Pallas kernels: 60.6 us -> 64.8 us
    pallas_call x1, Pallas kernels: 58.7 us -> 62.9 us  [shards(): pl.pallas_call(functools.partial(exchange_kernel, n, m, chunks, group_wid...]
where the time goes in v7:
time: 65.7 us; the launch traced here: 65.5 us
  Pallas kernels  64.8 us (99%)
    pallas_call x1, Pallas kernels, shards(): pl.pallas_call(functools.partial(exchange_kernel, n, m, chunks, group_wid...  62.9 us
    pallas_call x1, Pallas kernels, shards(): pl.pallas_call(scale_kernel, out_shape=(flat, flat, flat, jax.ShapeDtypeS...  1.9 us

profile of v7, /device:TPU:0, one launch (start us, length us, event | category | flops | bytes accessed | tf_op | source)
XLA Modules:
  0.0 65.5 jit_solution(4485394131301133000)
XLA Ops:
  0.6 62.9 %shard_map.101 = (f32[3,2048,256]{2,1,0:T(8,128)S(1)}, f32[8,16,128]{2,1,0:T(8,128)S(1)}, f32[8,256]{1,0:T(8,128)S(1)}) custom-call(bf16[8,256,256]{2,1,0:T(8,128)(2,1)} %bitcast.8, bf16[8,256,256]{2,1,0:T(8,128)(2,1)} %bitcast.9, bf16[8,256,256]{2,1,0:T(8,128)(2,1)} %bitcast.10, bf16[8,256,256]{2,1,0:T(8,128)(2,1)} %bitcast.11, s32[3,2,16]{2,1,0:T(2,128)} %bitcast.13, ...), custom_call_target="tpu_custom_call" | custom-call | tf_op jit(solution)/shard_map/pallas_call | solution.py:406
  63.6 1.9 %shard_map.102 = (bf16[2048,256]{1,0:T(8,128)(2,1)}, bf16[2048,256]{1,0:T(8,128)(2,1)}, bf16[2048,256]{1,0:T(8,128)(2,1)}, f32[8,16,128]{2,1,0:T(8,128)}, f32[2,3]{1,0:T(2,128)}) custom-call(f32[3,2048,256]{2,1,0:T(8,128)S(1)} %get-tuple-element.13.prod, f32[8,256]{1,0:T(8,128)S(1)} %get-tuple-element.14.peak, f32[8,16,128]{2,1,0:T(8,128)S(1)} %get-tuple-element.15.filt), custom_call_target="tpu_custom_call" | custom-call | tf_op jit(solution)/shard_map/pallas_call | solution.py:457
